TPU v7x, 32 devices: a whole 2x2x4 slice. The times are simulated.
32 devices in a mesh: rep: 8 (over z, y), grp: 4 (over x, core).
Axes of the slice: x: 2, y: 2, z: 4, core: 2. Of those that a mesh axis runs over, the one named last changes fastest.
Arguments:
- tokens: int32 [32, 1024], P(('rep', 'grp')), may hold values from 0 to 32
- mask: int32 [32, 1024], P(('rep', 'grp')), may hold values from 0 to 1, as said below
- targets: int32 [32, 1024], P(('rep', 'grp')), may hold values from 0 to 32
- mats_d: float32 [1, 480, 3840], P(None, 'grp')
- mats_down: float32 [1, 1920, 480], P(None, 'grp'), may hold values from -0.125 to 0.125
- mom_d: float32 [1, 480, 3840], P(None, 'grp'), may hold values from -4.5776367e-05 to 4.5776367e-05
- mom_down: float32 [1, 1920, 480], P(None, 'grp'), may hold values from -4.5776367e-05 to 4.5776367e-05
- err_d: float32 [8, 1, 480, 3840], P('rep', None, 'grp'), may hold values from -0.0009765625 to 0.0009765625
- err_down: float32 [8, 1, 1920, 480], P('rep', None, 'grp'), may hold values from -0.0009765625 to 0.0009765625
- q_d: float32 [1, 3840, 8], replicated, may hold values from -5 to 5
- q_down: float32 [1, 480, 8], replicated, may hold values from -5 to 5
- vectors: float32 [1, 6240], replicated
- vec_mom: float32 [1, 6240], replicated, may hold values from -0.00021362305 to 0.00021362305
- final_norm: float32 [2, 480], replicated
- final_mom: float32 [2, 480], replicated, may hold values from -0.00021362305 to 0.00021362305
- embed: float32 [33, 480], replicated, may hold values from -5 to 5
- embed_mom: float32 [33, 480], replicated, may hold values from -9.1552734e-05 to 9.1552734e-05
- head: float32 [481, 33], replicated, may hold values from -0.25 to 0.25
- head_mom: float32 [481, 33], replicated, may hold values from -9.1552734e-05 to 9.1552734e-05
Outputs:
- loss_sum: float32 [], replicated
- count: float32 [], replicated
- grad_norm: float32 [], replicated
- new_mats_d: float32 [1, 480, 3840], P(None, 'grp')
- new_mats_down: float32 [1, 1920, 480], P(None, 'grp')
- new_mom_d: float32 [1, 480, 3840], P(None, 'grp')
- new_mom_down: float32 [1, 1920, 480], P(None, 'grp')
- new_err_d: float32 [8, 1, 480, 3840], P('rep', None, 'grp')
- new_err_down: float32 [8, 1, 1920, 480], P('rep', None, 'grp')
- p_d: float32 [1, 480, 8], P(None, 'grp')
- p_down: float32 [1, 1920, 8], P(None, 'grp')
- new_q_d: float32 [1, 3840, 8], replicated
- new_q_down: float32 [1, 480, 8], replicated
- new_vectors: float32 [1, 6240], replicated
- new_vec_mom: float32 [1, 6240], replicated
- new_final_norm: float32 [2, 480], replicated
- new_final_mom: float32 [2, 480], replicated
- new_embed: float32 [33, 480], replicated
- new_embed_mom: float32 [33, 480], replicated
- new_head: float32 [481, 33], replicated
- new_head_mom: float32 [481, 33], replicated
Inputs may be any that keep to these rules, and one draw needn't show every extreme that they name: `mask`: position 0 of every sequence counts.
All inputs are finite; a program needn't handle non-finite values.
Results may differ from a plain program's by a relative error of at most 0.015.
The roundings to bfloat16 on the way count: a program that leaves them out, or rounds other values in their place, can miss the bound.
Values may be sent and summed in bfloat16 or wider, within the bound.
No kernel may reach another device: no remote copies, remote signals or barrier semaphores. Data moves between devices by JAX's collectives and lax.ppermute only.
A program may use at most 320 MiB of HBM per device.

v0:
```python
from functools import partial

import jax
import jax.numpy as jnp
import numpy as np
from jax import lax
from jax.experimental import pallas as pl
from jax.experimental.pallas import tpu as pltpu
from jax.sharding import PartitionSpec as P

D = 480
HEADS = 20
HDIM = 24
V = 33
PAD = 32
TOK = 40
WIDE = 512
EPS = 1e-05
BETA = 0.9
RATE_WIDE = 20000.0
RATE_LOWER = 3000.0
RATE_VECTOR = 20000.0
RATE_FINAL = 40000.0
RATE_EMBED = 60000.0
RATE_HEAD = 3000.0
CLIP = 0.005
F32 = jnp.float32
B16 = jnp.bfloat16
MIB = 2**20


ROOM = {
    "error_sketch": 16, "embed": 16, "project": 24, "attend": 30, "feed_and_loss": 56, "attend_back": 30,
    "input_grads": 30, "left_factors": 24, "merge_down": 12, "merge_rest": 16, "merge_in": 16, "finish": 30,
}


def params(name):
    return pltpu.CompilerParams(vmem_limit_bytes=ROOM[name] * MIB)


def nn(left, right):
    return jnp.dot(left, right, preferred_element_type=F32)


def nt(left, right):
    return lax.dot_general(left, right, (((1,), (1,)), ((), ())), preferred_element_type=F32)


def tn(left, right):
    return lax.dot_general(left, right, (((0,), (0,)), ((), ())), preferred_element_type=F32)


def thirds(value):
    top = value.astype(B16)
    rest = value - top.astype(F32)
    middle = rest.astype(B16)
    return top, middle, (rest - middle.astype(F32)).astype(B16)


def thirds_rows(value):
    return jnp.concatenate([part.astype(F32) for part in thirds(value)], 0).astype(B16)


def fold_rows(value):
    return value[0:8] + value[8:16] + value[16:24]


def exact_nt(left, right):
    return lax.dot_general(
        left, right, (((1,), (1,)), ((), ())),
        precision=lax.Precision.HIGHEST, preferred_element_type=F32,
    )


def exact_nn(left, right):
    return jnp.dot(left, right, precision=lax.Precision.HIGHEST, preferred_element_type=F32)


def three_nt(left, right):
    three = thirds_rows(left)
    top, middle, low = thirds(right)
    return fold_rows(nt(three, top) + nt(three, middle) + nt(three, low))


def three_nn(left, right):
    three = thirds_rows(left)
    top, middle, low = thirds(right)
    return fold_rows(nn(three, top) + nn(three, middle) + nn(three, low))


def norm_parts(value):
    center = value - jnp.mean(value, -1, keepdims=True)
    spread = jnp.mean(center * center, -1, keepdims=True)
    rstd = lax.rsqrt(spread + EPS)
    return center * rstd, rstd


def norm_back(grad, unit, rstd, gain):
    inner = grad * gain
    first = jnp.mean(inner, -1, keepdims=True)
    second = jnp.mean(inner * unit, -1, keepdims=True)
    return (
        rstd * (inner - first - unit * second),
        jnp.sum(grad * unit, 0, keepdims=True),
        jnp.sum(grad, 0, keepdims=True),
    )


def half_turn(value):
    return jnp.concatenate([value[HDIM // 2 :], value[: HDIM // 2]], 0)


def tail(rows, cols, ones):
    index = lax.broadcasted_iota(jnp.int32, (rows, cols), 0)
    return jnp.where(index < ones, 1.0, 0.0).astype(F32)


def lane_tail(rows, cols):
    index = lax.broadcasted_iota(jnp.int32, (rows, cols), 1)
    return jnp.where(index == 0, 1.0, 0.0).astype(F32)


def tables(length):
    half = HDIM // 2
    freq = np.float32(10000.0) ** (-np.arange(half, dtype=np.float32) * np.float32(2.0) / np.float32(HDIM))
    angle = np.arange(length, dtype=np.float32)[None, :] * freq.astype(np.float32)[:, None]
    cosine, sine = np.cos(angle), np.sin(angle)
    return (
        jnp.asarray(np.concatenate([cosine, cosine], 0), F32),
        jnp.asarray(np.concatenate([-sine, sine], 0), F32),
    )


def error_kernel(group, err_ref, errd_ref, q_ref, qd_ref, out_ref, row_ref):
    rows = err_ref.shape[0]
    out_ref[...] = jnp.zeros_like(out_ref)
    row_ref[...] = jnp.zeros_like(row_ref)
    row_ref[:, 0:rows] = three_nt(q_ref[...], err_ref[...])
    out_ref[0:8, :] = pltpu.roll(row_ref[...], rows * group[0], 1)
    start = pl.multiple_of(8 + 8 * group[0], 8)
    out_ref[pl.ds(start, 8), 0:D] = three_nt(qd_ref[...], errd_ref[...])


def embed_kernel(tok_ref, emb_ref, vec_ref, x_ref, h_ref, ht_ref, emb_s):
    step = tok_ref.shape[1]

    @pl.when(pl.program_id(0) == 0)
    def _():
        emb_s[...] = jnp.zeros_like(emb_s)
        emb_s[0:V, :] = emb_ref[...]

    index = lax.broadcasted_iota(jnp.int32, (TOK, step), 0)
    hot = jnp.where(index == tok_ref[...], 1.0, 0.0).astype(F32)
    hot = jnp.concatenate([hot, hot, hot], 0).astype(B16)
    x = tn(hot, thirds_rows(emb_s[...]))
    x_ref[...] = x
    unit, _ = norm_parts(x)
    normed = unit * vec_ref[:, 0:D] + vec_ref[:, D : 2 * D]
    h_ref[...] = normed.astype(B16)
    ht_ref[...] = jnp.concatenate([normed.T, tail(16, step, 1)], 0).astype(B16)


def spot(group, place, size, unit):
    return pl.ds(pl.multiple_of((group[0] ^ place) * size, unit), size)


def assemble(group, chunks, wide_s, out_s):
    for place, ref in enumerate(chunks):
        wide_s[spot(group, place, ref.shape[0], 8), :] = ref[...].astype(F32)
    out_s[...] = wide_s[...].astype(B16)


def project_kernel(members, group, h_ref, *refs):
    chunks = refs[:members]
    vec_ref, cos_ref, sin_ref, q_ref, k_ref, v_ref, wide_s, w_s = refs[members:]
    step = h_ref.shape[0]

    @pl.when(pl.program_id(0) == 0)
    def _():
        assemble(group, chunks, wide_s, w_s)

    act = nn(h_ref[...], w_s[...]) + vec_ref[:, 2 * D : 5 * D]
    turned = act.T
    cosine, sine = cos_ref[...], sin_ref[...]
    zeros = tail(PAD - HDIM, step, 0)
    ones = tail(PAD - HDIM, step, 3)
    for head in range(HEADS):
        low = HDIM * head
        query = turned[low : low + HDIM]
        query = (query * cosine + half_turn(query) * sine) * HDIM ** (-0.5)
        q_ref[head] = jnp.concatenate([query, zeros], 0).astype(B16)
        keys = turned[D + low : D + low + HDIM]
        keys = keys * cosine + half_turn(keys) * sine
        k_ref[head] = jnp.concatenate([keys, ones], 0).astype(B16)
        value = turned[2 * D + low : 2 * D + low + HDIM]
        v_ref[head] = jnp.concatenate([value, ones], 0).astype(B16)


def rows_of(value):
    return value.astype(F32).T.astype(B16)


def attend_kernel(q_ref, k_ref, v_ref, *refs):
    mix_ref, inv_ref, p_ref = refs[-3:]
    count, _, length = q_ref.shape
    zeros = tail(PAD - HDIM - 3, length, 0)

    def first(head):
        keys = rows_of(k_ref[head])
        query = q_ref[head]
        top = jnp.max(nn(keys, query), 0, keepdims=True)
        parts = [part.astype(F32) for part in thirds(-top)]
        return keys, jnp.concatenate([query[0:HDIM].astype(F32)] + parts + [zeros], 0).astype(B16)

    def second(head, keys, query):
        probs = jnp.exp(nn(keys, query)).astype(B16)
        p_ref[head] = probs
        out = nn(v_ref[head], probs)
        inverse = 1.0 / out[HDIM : HDIM + 1]
        mix_ref[HDIM * head : HDIM * head + HDIM, :] = out[0:HDIM] * inverse
        inv_ref[head] = inverse

    held = first(0)
    for head in range(count):
        ahead = first(head + 1) if head + 1 < count else None
        second(head, *held)
        held = ahead


def gelu_parts(upper):
    size = jnp.abs(upper) * (0.5**0.5)
    bell = jnp.exp(-0.5 * upper * upper)
    t = 1.0 / (1.0 + 0.3275911 * size)
    poly = t * (0.254829592 + t * (-0.284496736 + t * (1.421413741 + t * (-1.453152027 + t * 1.061405429))))
    lower = 0.5 * poly * bell
    cdf = jnp.where(upper < 0, lower, 1.0 - lower)
    return upper * cdf, cdf + upper * (0.3989422804014327 * bell)


def middle_kernel(members, group, mixa_ref, mixb_ref, inva_ref, invb_ref, x_ref, mask_ref, tgt_ref,
                  count_ref, vec_ref, fin_ref, head_ref, q_ref, qd_ref, *refs):
    chunks, chunks_down, refs = refs[:members], refs[members : 2 * members], refs[2 * members :]
    dm_ref, dx_ref, s_ref, e_ref, *refs = refs
    outs, outs_down, refs = refs[:members], refs[members : 2 * members], refs[2 * members :]
    acc_o, acc_u, acc_d, head_s, hid_s, slope_s, wide_s, wr_ref, wd_ref = refs
    pid = pl.program_id(0)
    step = x_ref.shape[0]
    wide = wd_ref.shape[0]
    wo = slice(wide, wide + D)

    @pl.when(pid == 0)
    def _():
        acc_o[...] = jnp.zeros_like(acc_o)
        acc_u[...] = jnp.zeros_like(acc_u)
        acc_d[...] = jnp.zeros_like(acc_d)
        e_ref[...] = jnp.zeros_like(e_ref)
        s_ref[...] = jnp.zeros_like(s_ref)
        head_s[...] = jnp.zeros_like(head_s)
        head_s[0:V, 0 : D + 1] = head_ref[...]
        assemble(group, chunks, wide_s, wr_ref)
        for place, ref in enumerate(chunks_down):
            wd_ref[spot(group, place, ref.shape[0], 16), :] = ref[...]

    mix = jnp.concatenate([mixa_ref[...], mixb_ref[...]], 0)
    half = inva_ref.shape[0]
    mixed = jnp.concatenate([mix, tail(16, step, 1)], 0).astype(B16)
    middle = x_ref[...] + tn(mixed[0:D], wr_ref[:, wo]) + vec_ref[:, 5 * D : 6 * D]
    unit2, rstd2 = norm_parts(middle)
    gain2 = vec_ref[:, 6 * D : 7 * D]
    normed2 = unit2 * gain2 + vec_ref[:, 7 * D : 8 * D]
    normed2 = jnp.concatenate([normed2, lane_tail(step, WIDE - D)], 1).astype(B16)
    bias_up = vec_ref[:, 9 * D :]
    block = 384
    for low in range(0, wide, block):
        cut = slice(low, low + block)
        upper = nn(normed2[:, 0:D], wr_ref[:, cut]) + bias_up[:, cut]
        hidden, slope = gelu_parts(upper)
        hid_s[:, cut] = hidden.astype(B16)
        slope_s[:, cut] = slope
    resid = middle + nn(hid_s[...], wd_ref[...]) + vec_ref[:, 8 * D : 9 * D]
    unit3, rstd3 = norm_parts(resid)
    final = unit3 * fin_ref[0:1, :] + fin_ref[1:2, :]
    final = jnp.concatenate([final, lane_tail(step, WIDE - D)], 1).astype(B16)

    lanes = lax.broadcasted_iota(jnp.int32, (TOK, WIDE), 1)
    bias = jnp.sum(jnp.where(lanes == D, head_s[...], 0.0), 1, keepdims=True)
    table = head_s[:, 0:D].astype(B16)
    rows = lax.broadcasted_iota(jnp.int32, (TOK, step), 0)
    logits = jnp.where(rows < V, nt(table, final[:, 0:D]) + bias, -1e30)
    shifted = logits - jnp.max(logits, 0, keepdims=True)
    expo = jnp.exp(shifted)
    total = jnp.sum(expo, 0, keepdims=True)
    picks = rows == tgt_ref[...]
    weight = mask_ref[...].astype(F32)
    picked = jnp.sum(jnp.where(picks, shifted, 0.0), 0, keepdims=True)
    loss = jnp.sum((jnp.log(total) - picked) * weight, 1, keepdims=True)
    grad_logits = (expo / total - jnp.where(picks, 1.0, 0.0)) * (weight * (1.0 / count_ref[0:1, 0:1]))
    grad_logits = grad_logits.astype(B16)
    e_ref[16 : 16 + TOK, :] += nn(grad_logits, final)
    grad_resid, grad_fg, grad_fb = norm_back(tn(grad_logits, table), unit3, rstd3, fin_ref[0:1, :])

    grad_y = grad_resid.astype(B16)
    acc_d[...] += tn(hid_s[...], grad_y)
    for low in range(0, wide, block):
        cut = slice(low, low + block)
        grad_hidden = nt(grad_y, wd_ref[cut, :])
        hid_s[:, cut] = (grad_hidden * slope_s[:, cut]).astype(B16)
    acc_u[...] += tn(normed2, hid_s[...])
    grad_mid, grad_g2, grad_b2 = norm_back(nt(hid_s[...], wr_ref[:, 0:wide]), unit2, rstd2, gain2)
    grad_mid = grad_mid + grad_resid
    dx_ref[...] = grad_mid
    branch = grad_mid.astype(B16)
    acc_o[...] += nn(mixed, branch)
    grad_mixed = nt(wr_ref[:, wo], branch).astype(B16).astype(F32)
    zeros = tail(PAD - HDIM - 3, step, 0)
    for head in range(HEADS):
        cut = slice(HDIM * head, HDIM * head + HDIM)
        inverse = inva_ref[head] if head < half else invb_ref[head - half]
        scaled = (grad_mixed[cut] * inverse).astype(B16).astype(F32)
        delta = -jnp.sum(scaled * mix[cut], 0, keepdims=True)
        top, mid, low = thirds(delta)
        dm_ref[head] = jnp.concatenate(
            [scaled, top.astype(F32), mid.astype(F32), low.astype(F32), zeros], 0
        ).astype(B16)
    e_ref[1:2, 0:D] += grad_g2
    e_ref[2:3, 0:D] += grad_b2
    e_ref[3:4, 0:D] += jnp.sum(grad_y.astype(F32), 0, keepdims=True)
    e_ref[8:9, 0:D] += grad_fg
    e_ref[9:10, 0:D] += grad_fb
    e_ref[10:11, :] += jnp.broadcast_to(loss, (1, WIDE))

    @pl.when(pid == pl.num_programs(0) - 1)
    def _():
        e_ref[0:1, 0:D] = acc_o[D : D + 1, :]
        for part in range(wide // D):
            e_ref[4 + part : 5 + part, 0:D] = acc_u[D : D + 1, D * part : D * part + D]
        go = acc_o[0:D, :].astype(B16)
        gu = acc_u[0:D, :].astype(B16)
        sketch = nt(thirds_rows(q_ref[:, 3 * D : 4 * D]), go) + nt(thirds_rows(q_ref[:, 4 * D :]), gu)
        s_ref[0:8, 0:D] = fold_rows(sketch)
        start = thirds_rows(qd_ref[...])
        for part in range(wide // D):
            piece = nt(start, acc_d[D * part : D * part + D, :].astype(B16))
            s_ref[8 + 8 * part : 16 + 8 * part, 0:D] = fold_rows(piece)
        for place, ref in enumerate(outs):
            at = spot(group, place, ref.shape[0], 8)
            ref[:, 0:wide] = acc_u[at, :].astype(B16)
            ref[:, wo] = acc_o[at, :].astype(B16)
        for place, ref in enumerate(outs_down):
            ref[...] = acc_d[spot(group, place, ref.shape[0], 8), :].astype(B16)


def attend_back_kernel(p_ref, q_ref, k_ref, v_ref, dm_ref, cos_ref, sin_ref, da_ref):
    cosine, sine = cos_ref[...], sin_ref[...]
    parts = [[], [], []]
    for head in range(p_ref.shape[0]):
        probs = p_ref[head]
        grad = dm_ref[head]
        slope = nn(rows_of(v_ref[head]), grad)
        grad_scores = (probs.astype(F32) * slope).astype(B16)
        grad_value = nt(grad, probs)[0:HDIM]
        grad_keys = nt(q_ref[head], grad_scores)[0:HDIM]
        grad_query = nn(k_ref[head], grad_scores)[0:HDIM] * HDIM ** (-0.5)
        parts[0].append(grad_query * cosine + half_turn(grad_query * sine))
        parts[1].append(grad_keys * cosine + half_turn(grad_keys * sine))
        parts[2].append(grad_value)
    for index in range(3):
        da_ref[index] = jnp.concatenate(parts[index], 0).astype(B16)


def input_kernel(members, group, tok_ref, da_ref, h_ref, x_ref, dx_ref, vec_ref, q_ref,
                 s_ref, serr_ref, e_ref, *refs):
    chunks, refs = refs[:members], refs[members:]
    outs, pieces, refs = refs[:members], refs[members : 2 * members], refs[2 * members :]
    out_ref, acc_w, acc_e, wide_s, w_s = refs
    pid = pl.program_id(0)
    step = x_ref.shape[0]

    @pl.when(pid == 0)
    def _():
        acc_w[...] = jnp.zeros_like(acc_w)
        acc_e[...] = jnp.zeros_like(acc_e)
        out_ref[...] = jnp.zeros_like(out_ref)
        assemble(group, chunks, wide_s, w_s)

    da = da_ref[...].reshape(3 * D, step)
    acc_w[...] += nt(h_ref[...], da)
    grad = nn(w_s[...], da).T
    unit, rstd = norm_parts(x_ref[...])
    grad_x, grad_g, grad_b = norm_back(grad, unit, rstd, vec_ref[:, 0:D])
    grad_x = grad_x + dx_ref[...]
    index = lax.broadcasted_iota(jnp.int32, (TOK, step), 0)
    hot = jnp.where(index == tok_ref[...], 1.0, 0.0).astype(B16)
    for part in thirds(grad_x):
        acc_e[...] += nn(hot, part)
    out_ref[40:41, 0:D] += grad_g
    out_ref[41:42, 0:D] += grad_b

    @pl.when(pid == pl.num_programs(0) - 1)
    def _():
        for part in range(3):
            out_ref[42 + part : 43 + part, 0:D] = acc_w[D : D + 1, D * part : D * part + D]
        out_ref[0:40, :] = s_ref[...] + serr_ref[...]
        out_ref[0:8, 0:D] += fold_rows(nt(thirds_rows(q_ref[:, 0 : 3 * D]), acc_w[0:D, :].astype(B16)))
        out_ref[45:48, :] = e_ref[8:11, :]
        out_ref[48:56, :] = e_ref[0:8, :]
        out_ref[56 : 56 + V, 0:D] = acc_e[0:V, :]
        out_ref[56 + V : 56 + 2 * V, :] = e_ref[16 : 16 + V, :]
        for place, ref in enumerate(outs):
            ref[...] = acc_w[spot(group, place, ref.shape[0], 8), :].astype(B16)
        for place, ref in enumerate(pieces):
            ref[...] = out_ref[spot(group, place, ref.shape[0], 8), :]


def orthonormal(sketch, gram):
    basis = jnp.zeros_like(sketch[0])
    count = gram.shape[0]
    index = lax.broadcasted_iota(jnp.int32, (count, 1), 0)
    out = [jnp.zeros_like(part) for part in sketch]
    left = list(sketch)
    for step in range(count):
        pivot = gram[step : step + 1, step : step + 1]
        scale = 1.0 / jnp.sqrt(pivot)
        column = gram[:, step : step + 1] * scale
        row = gram[step : step + 1, :] * scale
        column = jnp.where(index > step, column, 0.0)
        gram = gram - column * row
        for place in range(len(left)):
            base = left[place][step : step + 1, :] * scale
            out[place] = jnp.where(index == step, base, out[place])
            left[place] = left[place] - column * base
    return out


def factor_kernel(members, group, *refs):
    chunks, ins, rests, downs = (refs[members * part : members * part + members] for part in range(4))
    err_ref, errd_ref, a_ref, p_ref, own_ref, ownd_ref, *refs = refs[4 * members :]
    outs, f_s = refs[:members], refs[members]
    rows, wide_cols = err_ref.shape
    hidden = wide_cols - 4 * D
    parts = hidden // D
    for place, ref in enumerate(chunks):
        a_ref[spot(group, place, ref.shape[0], 8), :] = ref[...]
    wide = a_ref[0:8, 0:D]
    down = [a_ref[8 + 8 * part : 16 + 8 * part, 0:D] for part in range(parts)]
    gram = exact_nt(wide, wide)
    (wide,) = orthonormal([wide], gram)
    gram = exact_nt(down[0], down[0])
    for part in range(1, parts):
        gram = gram + exact_nt(down[part], down[part])
    down = orthonormal(down, gram)
    p_ref[...] = jnp.zeros_like(p_ref)
    p_ref[0:8, 0:D] = wide
    for part in range(parts):
        p_ref[8 + 8 * part : 16 + 8 * part, 0:D] = down[part]
    f_s[...] = jnp.zeros_like(f_s)
    for place in range(members):
        piece = pltpu.roll(p_ref[0:8, :], (WIDE - rows * (group[0] ^ place)) % WIDE, 1)[:, 0:rows]
        piece_down = p_ref[pl.ds(pl.multiple_of(8 + 8 * (group[0] ^ place), 8), 8), :][:, 0:D]
        if place == 0:
            own_ref[...] = piece
            ownd_ref[...] = piece_down
            f_s[:, 0:wide_cols] = three_nn(piece, err_ref[...])
            f_s[:, wide_cols : wide_cols + D] = three_nn(piece_down, errd_ref[...])
        three = thirds_rows(piece)
        f_s[:, 0 : 3 * D] += fold_rows(nn(three, ins[place][...]))
        f_s[:, 4 * D : wide_cols] += fold_rows(nn(three, rests[place][:, 0:hidden]))
        f_s[:, 3 * D : 4 * D] += fold_rows(nn(three, rests[place][:, hidden:]))
        f_s[:, wide_cols : wide_cols + D] += fold_rows(nn(thirds_rows(piece_down), downs[place][...]))
    for place, ref in enumerate(outs):
        ref[...] = f_s[:, spot(group, place, ref.shape[1], 128)]


def merge_kernel(*refs):
    *chunks, err_ref, out_ref = refs
    value = err_ref[...]
    for ref in chunks:
        value = value + ref[...].astype(F32)
    out_ref[...] = value


def merge_rest_kernel(*refs):
    *chunks, err_ref, out_ref = refs
    value = chunks[0][...].astype(F32)
    for ref in chunks[1:]:
        value = value + ref[...].astype(F32)
    hidden = value.shape[1] - D
    out_ref[:, 0:hidden] = value[:, 0:hidden] + err_ref[:, 4 * D :]
    out_ref[:, hidden:] = value[:, hidden:] + err_ref[:, 3 * D : 4 * D]


def merge_in_kernel(*refs):
    *chunks, err_ref, out_ref = refs
    value = err_ref[:, 0 : 3 * D]
    for ref in chunks:
        value = value + ref[...].astype(F32)
    out_ref[...] = value


def six(left, right):
    first, second = thirds(left), thirds(right)
    order = ((0, 0), (0, 1), (1, 0), (1, 1), (0, 2), (2, 0))
    left = jnp.concatenate([first[i].astype(F32) for i, _ in order], 0).astype(B16)
    right = jnp.concatenate([second[j].astype(F32) for _, j in order], 0).astype(B16)
    return tn(left, right)


def renew(weight, moment, grad, scale, rate):
    new_moment = BETA * moment + scale * grad
    return weight - rate * new_moment, new_moment


def finish_kernel(members, replicas, group, *refs):
    chunks, rest = refs[:members], refs[members:]
    (a_ref, p_ref, own_ref, ownd_ref,
     w_ref, wd_ref, m_ref, md_ref, ein_ref, erest_ref, errd_ref, count_ref,
     vec_ref, vmom_ref, fin_ref, fmom_ref, emb_ref, emom_ref, head_ref, hmom_ref,
     loss_ref, total_ref, norm_ref, nq_ref, nqd_ref, nw_ref, nwd_ref, nm_ref, nmd_ref, ne_ref, ned_ref,
     nvec_ref, nvmom_ref, nfin_ref, nfmom_ref, nemb_ref, nemom_ref, nhead_ref, nhmom_ref, f_s) = rest
    wide_cols = w_ref.shape[1]
    hidden = wide_cols - 4 * D
    for place, ref in enumerate(chunks):
        f_s[:, spot(group, place, ref.shape[1], 128)] = ref[...]
    factor, factor_down = f_s[:, 0:wide_cols], f_s[:, wide_cols : wide_cols + D]
    nq_ref[...] = factor
    nqd_ref[...] = factor_down
    a = a_ref[...]
    square = jnp.sum(a[40:47, 0:D] * a[40:47, 0:D]) + jnp.sum(a[48:56, 0:D] * a[48:56, 0:D])
    emb, top = a[56 : 56 + V, 0:D], a[56 + V : 56 + 2 * V, 0 : D + 1]
    square = square + jnp.sum(emb * emb) + jnp.sum(top * top)
    basis = p_ref[...]
    gram = exact_nt(basis[0:8, 0:D], basis[0:8, 0:D])
    square = square + jnp.sum(gram * exact_nt(factor, factor))
    gram = jnp.zeros((8, 8), F32)
    for part in range(1, basis.shape[0] // 8):
        piece = basis[8 * part : 8 * part + 8, 0:D]
        gram = gram + exact_nt(piece, piece)
    square = square + jnp.sum(gram * exact_nt(factor_down, factor_down))
    norm = jnp.sqrt(square)
    norm_ref[...] = jnp.broadcast_to(norm, norm_ref.shape)
    loss_ref[...] = a[47:48, 0:1]
    total_ref[...] = count_ref[0:1, 0:1]
    scale = jnp.minimum(1.0, CLIP / norm)

    approx = six(own_ref[...], factor)
    nw_ref[...], nm_ref[...] = renew(w_ref[...], m_ref[...], approx, scale, RATE_WIDE)
    share = approx * (1.0 / replicas)
    ne_ref[:, 0 : 3 * D] = ein_ref[...] - share[:, 0 : 3 * D]
    ne_ref[:, 3 * D : 4 * D] = erest_ref[:, hidden:] - share[:, 3 * D : 4 * D]
    ne_ref[:, 4 * D :] = erest_ref[:, 0:hidden] - share[:, 4 * D :]
    approx = six(ownd_ref[...], factor_down)
    nwd_ref[...], nmd_ref[...] = renew(wd_ref[...], md_ref[...], approx, scale, RATE_LOWER)
    ned_ref[...] = errd_ref[...] - approx * (1.0 / replicas)

    places = (40, 41, 42, 43, 44, 48, 49, 50, 51, 52, 53, 54, 55)
    for row, place in enumerate(places):
        cut = slice(D * row, D * row + D)
        nvec_ref[:, cut], nvmom_ref[:, cut] = renew(
            vec_ref[:, cut], vmom_ref[:, cut], a[place : place + 1, 0:D], scale, RATE_VECTOR
        )
    nfin_ref[...], nfmom_ref[...] = renew(fin_ref[...], fmom_ref[...], a[45:47, 0:D], scale, RATE_FINAL)
    nemb_ref[...], nemom_ref[...] = renew(emb_ref[...], emom_ref[...], emb, scale, RATE_EMBED)
    nhead_ref[...], nhmom_ref[...] = renew(head_ref[...], hmom_ref[...], top, scale, RATE_HEAD)


def swap(value, axis, bit):
    size = lax.axis_size(axis)
    return lax.ppermute(value, axis, [(i, i ^ bit) for i in range(size)])


def bits_of(axis):
    size, bit, out = lax.axis_size(axis), 1, []
    while bit < size:
        out.append(bit)
        bit *= 2
    return out


def tie(*values):
    return lax.optimization_barrier(values)


def send_chunks(pieces):
    return [pieces[0]] + [swap(piece, "grp", place) for place, piece in enumerate(pieces) if place]


def add_chunks(pieces, work=()):
    work, results = dict(work), {}

    def beside(turn, moved):
        if turn in work:
            moved, results[turn] = tie(moved, work[turn]())
        return moved

    got = beside(0, send_chunks(pieces))
    total = got[0]
    for piece in got[1:]:
        total = total + piece
    for turn, bit in enumerate(bits_of("rep")):
        total = total + beside(turn + 1, swap(total, "rep", bit))
    got = [total] + [swap(total, "grp", place) for place in range(1, len(pieces))]
    return beside(-1, got), results


def gather_start(value):
    first, *bits = reversed(bits_of("grp"))
    return [value, swap(value, "grp", first)]


def gather_end(pieces):
    first, *bits = reversed(bits_of("grp"))
    order = [0, first]
    for bit in bits:
        pieces = pieces + [swap(piece, "grp", bit) for piece in pieces]
        order = order + [place ^ bit for place in order]
    return [pieces[order.index(place)] for place in range(len(order))]


def halve_start(pieces):
    first, *bits = bits_of("grp")
    keep = [place for place in range(len(pieces)) if not place & first]
    return [(place, pieces[place], swap(pieces[place | first], "grp", first)) for place in keep]


def halve_end(pairs):
    first, *bits = bits_of("grp")
    (_, own, other), *others = pairs
    kept = [own, other]
    sums = {place: (mine.astype(F32) + theirs.astype(F32)).astype(B16) for place, mine, theirs in others}
    for bit in bits:
        kept.append(swap(sums[bit], "grp", bit))
        sums = {
            place: (sums[place].astype(F32) + swap(sums[place | bit], "grp", bit).astype(F32)).astype(B16)
            for place in sums
            if not place & bit
        }
    return kept


def whole(shape):
    return pl.BlockSpec(shape, lambda *_: (0,) * len(shape))


def shards(tokens, mask, targets, mats_d, mats_down, mom_d, mom_down, err_d, err_down, q_d, q_down,
           vectors, vec_mom, final_norm, final_mom, embed, embed_mom, head, head_mom):
    length = tokens.shape[1]
    wide = mats_d.shape[2]
    hidden = wide - 4 * D
    rows = mats_d.shape[1]
    rows_down = mats_down.shape[1]
    step = 256
    steps = length // step
    step_mid = 2 * step
    index = lax.axis_index("grp").astype(jnp.int32)
    group = index.reshape(1)
    members = lax.axis_size("grp")
    cosine, sine = tables(length)
    q_t, qd_t = q_d[0].T, q_down[0].T
    head_t = head.T
    err, errd = err_d[0, 0], err_down[0, 0]

    def call(kernel, name, grid, ins, outs, shapes, scratch=()):
        return pl.pallas_call(
            kernel,
            grid_spec=pltpu.PrefetchScalarGridSpec(
                num_scalar_prefetch=1, grid=grid, in_specs=ins, out_specs=outs, scratch_shapes=scratch
            ),
            out_shape=shapes,
            compiler_params=params(name),
            name=name,
        )

    shape = jax.ShapeDtypeStruct
    rounds = [("grp", bit) for bit in bits_of("grp")] + [("rep", bit) for bit in bits_of("rep")]

    def advance(value, times=1):
        for _ in range(min(times, len(rounds))):
            value = value + swap(value, *rounds.pop(0))
        return value

    cols = pl.BlockSpec((1, step), lambda i, *_: (0, i))
    flat = pl.BlockSpec((step, D), lambda i, *_: (i, 0))
    heads = pl.BlockSpec((HEADS, PAD, step), lambda i, *_: (0, 0, i))
    wave = pl.BlockSpec((HDIM, step), lambda i, *_: (0, i))
    ext = pl.BlockSpec((D + 16, step), lambda i, *_: (0, i))

    w_in = gather_start(mats_d[0][:, : 3 * D].astype(B16))
    counted = jnp.broadcast_to(jnp.sum(mask.astype(F32)), (8, 128))
    more = advance(counted)
    err_sketch = call(
        error_kernel, "error_sketch", (1,),
        [whole((rows, wide)), whole((rows_down, D)), whole((8, wide)), whole((8, D))],
        whole((40, WIDE)), shape((40, WIDE), F32), [pltpu.VMEM((8, WIDE), F32)],
    )(group, err, errd, q_t, qd_t)
    x, h, h_t = pl.pallas_call(
        embed_kernel,
        grid=(steps,),
        in_specs=[cols, whole((V, D)), whole(vectors.shape)],
        out_specs=[flat, flat, ext],
        out_shape=[shape((length, D), F32), shape((length, D), B16), shape((D + 16, length), B16)],
        scratch_shapes=[pltpu.VMEM((TOK, D), F32)],
        compiler_params=params("embed"),
        name="embed",
    )(tokens, embed, vectors)
    w_in, err_sketch, h, counted = tie(w_in, err_sketch, h, more)
    w_in = gather_end(w_in)
    rest = jnp.concatenate([mats_d[0][:, 4 * D :], mats_d[0][:, 3 * D : 4 * D]], 1).astype(B16)
    down = mats_down[0].astype(B16)
    more = advance(counted)
    w_in, counted, rest, down = tie(w_in, more, rest, down)
    w_rest, w_down = gather_start(rest), gather_start(down)
    more = advance(counted)
    query, keys, value = call(
        partial(project_kernel, members), "project", (steps,),
        [flat] + [whole((rows, 3 * D))] * members + [whole(vectors.shape), wave, wave],
        [heads] * 3, [shape((HEADS, PAD, length), B16)] * 3,
        [pltpu.VMEM((D, 3 * D), F32), pltpu.VMEM((D, 3 * D), B16)],
    )(group, h, *w_in, vectors, cosine, sine)
    query, counted = tie(query, more)

    half = HEADS // 2
    pair = 2
    turned = half // pair
    mixes, inverses, probs = [], [], []
    for part in range(2):
        one = pl.BlockSpec((1, PAD, length), lambda i, part=part: (i + half * part, 0, 0))
        more = advance(counted, 1 + part * len(rounds))
        mix, inverse, *probs = pl.pallas_call(
            attend_kernel,
            grid=(half,),
            in_specs=[one, one, one] + [pl.BlockSpec(memory_space=pl.ANY)] * len(probs),
            out_specs=[
                pl.BlockSpec((HDIM, length), lambda i: (i, 0)),
                pl.BlockSpec((1, 1, length), lambda i: (i, 0, 0)),
                pl.BlockSpec((1, length, length), lambda i, part=part: (i + half * part, 0, 0)),
            ],
            out_shape=[
                shape((half * HDIM, length), F32),
                shape((half, 1, length), F32),
                shape((HEADS, length, length), B16),
            ],
            input_output_aliases={3: 2} if probs else {},
            compiler_params=params("attend"),
            name="attend",
        )(query, keys, value, *probs)
        mix, query, counted, w_rest, w_down = tie(mix, query, more, w_rest, w_down)
        if part == 0:
            w_rest, w_down = gather_end(w_rest), gather_end(w_down)
        mixes.append(mix)
        inverses.append(inverse)

    cols2 = pl.BlockSpec((1, step_mid), lambda i, *_: (0, i))
    flat2 = pl.BlockSpec((step_mid, D), lambda i, *_: (i, 0))
    heads2 = pl.BlockSpec((HEADS, PAD, step_mid), lambda i, *_: (0, 0, i))
    everyone = [(rows, D + hidden)] * members + [(rows_down, D)] * members
    grad_mix, grad_mid, sketch, early, *grads = call(
        partial(middle_kernel, members), "feed_and_loss", (length // step_mid,),
        [pl.BlockSpec((half * HDIM, step_mid), lambda i, *_: (0, i))] * 2
        + [pl.BlockSpec((half, 1, step_mid), lambda i, *_: (0, 0, i))] * 2
        + [
            flat2, cols2, cols2, whole((8, 128)), whole(vectors.shape), whole((2, D)),
            whole((V, D + 1)), whole((8, wide)), whole((8, D)),
        ]
        + [whole(item) for item in everyone],
        [heads2, flat2, whole((40, WIDE)), whole((56, WIDE))] + [whole(item) for item in everyone],
        [
            shape((HEADS, PAD, length), B16),
            shape((length, D), F32),
            shape((40, WIDE), F32),
            shape((56, WIDE), F32),
        ]
        + [shape(item, B16) for item in everyone],
        [
            pltpu.VMEM((D + 16, D), F32),
            pltpu.VMEM((WIDE, hidden), F32),
            pltpu.VMEM((hidden, D), F32),
            pltpu.VMEM((TOK, WIDE), F32),
            pltpu.VMEM((step_mid, hidden), B16),
            pltpu.VMEM((step_mid, hidden), F32),
            pltpu.VMEM((D, D + hidden), F32),
            pltpu.VMEM((D, D + hidden), B16),
            pltpu.VMEM((hidden, D), B16),
        ],
    )(group, *mixes, *inverses, x, mask, targets, counted, vectors, final_norm, head_t, q_t, qd_t,
      *w_rest, *w_down)
    g_rest, g_down = grads[:members], grads[members:]
    all_down = send_chunks(g_down)
    all_rest = send_chunks(g_rest)

    two = pl.BlockSpec((pair, PAD, length), lambda i: (i, 0, 0))
    grad_act = pl.pallas_call(
        attend_back_kernel,
        grid=(HEADS // pair,),
        in_specs=[
            pl.BlockSpec((pair, length, length), lambda i: (i, 0, 0)),
            two, two, two, two, whole((HDIM, length)), whole((HDIM, length)),
        ],
        out_specs=pl.BlockSpec((3, pair * HDIM, length), lambda i: (0, i, 0)),
        out_shape=shape((3, D, length), B16),
        compiler_params=params("attend_back"),
        name="attend_back",
    )(*probs, query, keys, value, grad_mix, cosine, sine)
    all_down, all_rest, grad_act = tie(all_down, all_rest, grad_act)

    act = pl.BlockSpec((3, D, step), lambda i, *_: (0, 0, i))
    size = 128 // members
    ins = [(rows, 3 * D)] * members
    grads = call(
        partial(input_kernel, members), "input_grads", (steps,),
        [
            cols, act, ext, flat, flat,
            whole(vectors.shape), whole((8, wide)), whole((40, WIDE)), whole((40, WIDE)), whole((56, WIDE)),
        ]
        + [whole(item) for item in ins],
        [whole(item) for item in ins] + [whole((size, WIDE))] * members,
        [shape(item, B16) for item in ins] + [shape((size, WIDE), F32)] * members,
        [
            pltpu.VMEM((128, WIDE), F32), pltpu.VMEM((D + 16, 3 * D), F32), pltpu.VMEM((TOK, D), F32),
            pltpu.VMEM((D, 3 * D), F32), pltpu.VMEM((D, 3 * D), B16),
        ],
    )(group, tokens, grad_act, h_t, x, grad_mid, vectors, q_t, sketch, err_sketch, early, *w_in)
    g_in, pieces = grads[:members], grads[members:]
    half_in = halve_start(g_in)

    def merge(kernel, name, chunks, err, result):
        return lambda: pl.pallas_call(
            kernel, out_shape=shape(result, F32), compiler_params=params(name), name=name
        )(*chunks, err)

    chunks, merged = add_chunks(
        pieces,
        (
            (0, merge(merge_kernel, "merge_down", all_down, errd, errd.shape)),
            (1, lambda: halve_end(half_in)),
            (2, merge(merge_rest_kernel, "merge_rest", all_rest, err, (rows, D + hidden))),
        ),
    )
    merged_down, all_in, merged_rest = (merged[turn] for turn in range(3))
    span = -(-(wide + WIDE) // (128 * members)) * 128
    shared, basis, own, ownd, *pieces = call(
        partial(factor_kernel, members), "left_factors", (1,),
        [whole((size, WIDE))] * members + [whole(item) for item in ins + everyone]
        + [whole((rows, wide)), whole((rows_down, D))],
        [whole((128, WIDE)), whole((40, WIDE)), whole((8, rows)), whole((8, rows_down))]
        + [whole((8, span))] * members,
        [
            shape((128, WIDE), F32), shape((40, WIDE), F32), shape((8, rows), F32), shape((8, rows_down), F32),
        ]
        + [shape((8, span), F32)] * members,
        [pltpu.VMEM((8, span * members), F32)],
    )(group, *chunks, *g_in, *g_rest, *g_down, err, errd)

    chunks, merged = add_chunks(
        pieces, ((0, merge(merge_in_kernel, "merge_in", all_in, err, (rows, 3 * D))),)
    )
    merged_in = merged[0]

    same = lambda value: shape(value.shape, F32)
    replicas = lax.axis_size("rep")
    small = (vectors, vec_mom, final_norm, final_mom, embed, embed_mom, head_t, head_mom.T)
    given = (
        *chunks, shared, basis, own, ownd,
        mats_d[0], mats_down[0], mom_d[0], mom_down[0], merged_in, merged_rest, merged_down, counted, *small,
    )
    shapes = [
        shape((1, 1), F32), shape((1, 1), F32), shape((1, 1), F32), shape((8, wide), F32), shape((8, D), F32),
        same(mats_d[0]), same(mats_down[0]), same(mats_d[0]), same(mats_down[0]), same(err), same(errd),
    ] + [same(item) for item in small]
    outs = call(
        partial(finish_kernel, members, replicas), "finish", (1,),
        [whole(item.shape) for item in given], [whole(item.shape) for item in shapes], shapes,
        [pltpu.VMEM((8, span * members), F32)],
    )(group, *given)
    (loss, total, norm, new_q, new_qd, new_wide, new_down, new_mom_wide, new_mom_dn, new_err, new_errd,
     new_vec, new_vmom, new_fin, new_fmom, new_emb, new_emom, new_head, new_hmom) = outs
    return (
        loss.reshape(()),
        total.reshape(()),
        norm.reshape(()),
        new_wide[None],
        new_down[None],
        new_mom_wide[None],
        new_mom_dn[None],
        new_err[None, None],
        new_errd[None, None],
        own.T[None],
        ownd.T[None],
        new_q.T[None],
        new_qd.T[None],
        new_vec,
        new_vmom,
        new_fin,
        new_fmom,
        new_emb,
        new_emom,
        new_head.T,
        new_hmom.T,
    )


def solution(mesh):
    whole_seq = P(("rep", "grp"), None)
    by_rows = P(None, "grp", None)
    by_replica = P("rep", None, "grp", None)
    placed = (
        (whole_seq,) * 3 + (by_rows,) * 4 + (by_replica,) * 2 + (P(),) * 10
    )
    given = (P(),) * 3 + (by_rows,) * 4 + (by_replica,) * 2 + (by_rows,) * 2 + (P(),) * 10
    return jax.shard_map(shards, mesh=mesh, in_specs=placed, out_specs=given, check_vma=False)
```

profile of v0, /device:TPU:0, one launch (start us, length us, event | category | flops | bytes accessed | tf_op | source)
XLA Modules:
  0.0 229.6 jit_solution(5246510879320887828)
XLA Ops:
  0.7 1.8 bitcast_convert_fusion.1
  2.5 3.0 %collective-permute-start = (bf16[120,1440]{1,0:T(8,128)(2,1)S(1)}, bf16[120,1440]{1,0:T(8,128)(2,1)}, u32[]{:S(2)}, u32[]{:S(2)}) collective-permute-start(bf16[120,1440]{1,0:T(8,128)(2,1)S(1)} %slice.15.refs_0_), channel_id=1, source_target_pairs={{0,2},{1,3},{2,0},{3,1},{4,6},{5,7},{6,4},{7,5},{8,10},{9,11},{10,... | collective-permute-start | bytes 1036808 | tf_op jit(solution)/shard_map/ppermute | solution.py:569
  5.6 0.6 convert_reduce_fusion
  6.2 0.6 broadcast_in_dim.33
  6.9 0.8 slice.17
  7.7 2.2 embed.1
  9.9 1.3 copy-done.2
  11.2 1.0 copy-done.14
  12.2 1.5 error_sketch.1.serr_ref
  13.7 0.7 broadcast_add_fusion
  14.4 0.6 collective-permute-start.2
  15.1 1.5 collective-permute-start.4
  16.7 2.1 collective-permute-done.4
  18.8 1.5 collective-permute-start.7
  20.3 0.6 collective-permute-start.8
  20.9 1.5 collective-permute-start.5
  22.4 4.7 %project.1 = (bf16[20,32,1024]{2,1,0:T(8,128)(2,1)S(1)}, bf16[20,32,1024]{2,1,0:T(8,128)(2,1)S(1)}, bf16[20,32,1024]{2,1,0:T(8,128)(2,1)S(1)}) custom-call(s32[1]{0:T(128)} %bitcast.group, bf16[1024,480]{1,0:T(8,128)(2,1)S(1)} %get-tuple-element.138.h_ref, bf16[120,1440]{1,0:T(8,128)(2,1)S(1)} %slice.15.refs_0_, ...), custom_call_target="tpu_custom_call" | custom-call | tf_op jit(solution)/shard_map/project/pallas_call | solution.py:714
  27.2 1.7 collective-permute-start.6
  28.8 17.7 %attend.2 = (f32[240,1024]{1,0:T(8,128)S(1)}, f32[10,1,1024]{2,1,0:T(1,128)S(1)}, bf16[20,1024,1024]{2,1,0:T(8,128)(2,1)}) custom-call(bf16[20,32,1024]{2,1,0:T(8,128)(2,1)S(1)} %get-tuple-element.186.q_ref, bf16[20,32,1024]{2,1,0:T(8,128)(2,1)S(1)} %get-tuple-element.149.k_ref, bf16[20,32,1024]{2,1,0:T(8,128)(2,1)S(1)} %get-tuple-element.150.v_ref), custom_call_target="tpu_custom_call" | custom-call | tf_op jit(solution)/shard_map/attend/pallas_call | solution.py:729
  46.5 0.6 copy-done.37
  47.2 0.5 collective-permute-start.11
  48.2 2.6 %collective-permute-start.9 = (f32[8,128]{1,0:T(8,128)S(1)}, f32[8,128]{1,0:T(8,128)S(1)}, u32[]{:S(2)}, u32[]{:S(2)}) collective-permute-start(f32[8,128]{1,0:T(8,128)S(1)} %add.57), channel_id=1, source_target_pairs={{0,16},{4,20},{8,24},{12,28},{16,0},{20,4},{24,8},{28,12},{1,17},{... | collective-permute-start | bytes 12296 | tf_op jit(solution)/shard_map/ppermute | solution.py:569
  50.8 17.7 %attend.3 = (f32[240,1024]{1,0:T(8,128)S(1)}, f32[10,1,1024]{2,1,0:T(1,128)S(1)}, bf16[20,1024,1024]{2,1,0:T(8,128)(2,1)}) custom-call(bf16[20,32,1024]{2,1,0:T(8,128)(2,1)S(1)} %get-tuple-element.186.q_ref, bf16[20,32,1024]{2,1,0:T(8,128)(2,1)S(1)} %get-tuple-element.149.k_ref, ...), custom_call_target="tpu_custom_call", output_to_operand_aliasing={{2}: (3, {})} | custom-call | tf_op jit(solution)/shard_map/attend/pallas_call | solution.py:729
  68.5 0.9 copy-done.18
  69.5 0.6 copy-done.38
  70.1 0.6 add.58.count_ref.refs_15_
  70.7 0.9 copy-done.50
  71.6 0.8 copy-done.51
  72.4 33.7 %feed_and_loss.1 = (bf16[20,32,1024]{2,1,0:T(8,128)(2,1)}, f32[1024,480]{1,0:T(8,128)}, f32[40,512]{1,0:T(8,128)}, f32[56,512]{1,0:T(8,128)}, bf16[120,2400]{1,0...) custom-call(s32[1]{0:T(128)} %bitcast.group, ...), custom_call_target="tpu_custom_call" | custom-call | tf_op jit(solution)/shard_map/feed_and_loss/pallas_call | solution.py:757
  106.2 0.5 collective-permute-start.17
  106.7 1.5 collective-permute-start.18
  108.1 1.4 collective-permute-start.15
  109.5 0.6 collective-permute-start.16
  110.2 1.3 copy-done.11
  111.5 46.0 %attend_back.1.da_ref = bf16[3,480,1024]{2,1,0:T(8,128)(2,1)S(1)} custom-call(bf16[20,1024,1024]{2,1,0:T(8,128)(2,1)} %get-tuple-element.185.p_ref, bf16[20,32,1024]{2,1,0:T(8,128)(2,1)S(1)} %get-tuple-element.186.q_ref, bf16[20,32,1024]{2,1,0:T(8,128)(2,1)S(1)} %get-tuple-element.149.k_ref, bf16[20,32,1024]{2,1,0:T(8,128)(2,1)S(1)} %get-tuple-element.150.v_ref, ...), custom_call_target="tpu_custom_call" | custom-call | tf_op jit(solution)/shard_map/attend_back/pallas_call | solution.py:792
  157.6 9.8 %input_grads.1 = (bf16[120,1440]{1,0:T(8,128)(2,1)S(1)}, bf16[120,1440]{1,0:T(8,128)(2,1)S(1)}, bf16[120,1440]{1,0:T(8,128)(2,1)S(1)}, bf16[120,1440]{1,0:T(8,12...) custom-call(s32[1]{0:T(128)} %bitcast.group, ...), custom_call_target="tpu_custom_call" | custom-call | tf_op jit(solution)/shard_map/input_grads/pallas_call | solution.py:809
  168.1 1.5 collective-permute-start.21
  169.6 0.6 collective-permute-start.24
  170.3 1.5 collective-permute-start.26
  172.3 1.6 collective-permute-done.22
  173.9 0.6 collective-permute-start.23
  174.5 3.8 %collective-permute-done.23 = f32[32,512]{1,0:T(8,128)S(1)} collective-permute-done((f32[32,512]{1,0:T(8,128)S(1)}, f32[32,512]{1,0:T(8,128)S(1)}, u32[]{:S(2)}, u32[]{:S(2)}) %collective-permute-start.23) | collective-permute-done | bytes 65568 | tf_op jit(solution)/shard_map/ppermute | solution.py:569
  178.3 3.5 %collective-permute-done.26.refs_2_ = bf16[120,1440]{1,0:T(8,128)(2,1)S(1)} collective-permute-done((bf16[120,1440]{1,0:T(8,128)(2,1)S(1)}, bf16[120,1440]{1,0:T(8,128)(2,1)S(1)}, u32[]{:S(2)}, u32[]{:S(2)}) %collective-permute-start.26) | collective-permute-done | bytes 345632 | tf_op jit(solution)/shard_map/ppermute | solution.py:569
  181.9 0.5 collective-permute-start.27
  182.4 0.6 merge_rest.1.refs_13_
  183.0 3.2 %collective-permute-done.27 = f32[32,512]{1,0:T(8,128)S(1)} collective-permute-done((f32[32,512]{1,0:T(8,128)S(1)}, f32[32,512]{1,0:T(8,128)S(1)}, u32[]{:S(2)}, u32[]{:S(2)}) %collective-permute-start.27) | collective-permute-done | bytes 65568 | tf_op jit(solution)/shard_map/ppermute | solution.py:569
  186.6 5.4 %collective-permute-done.28 = f32[32,512]{1,0:T(8,128)S(1)} collective-permute-done((f32[32,512]{1,0:T(8,128)S(1)}, f32[32,512]{1,0:T(8,128)S(1)}, u32[]{:S(2)}, u32[]{:S(2)}) %collective-permute-start.28) | collective-permute-done | bytes 65568 | tf_op jit(solution)/shard_map/ppermute | solution.py:569
  192.1 1.4 collective-permute-start.30
  193.5 0.5 collective-permute-start.31
  194.0 2.9 %collective-permute-done.30.refs_2_ = f32[32,512]{1,0:T(8,128)S(1)} collective-permute-done((f32[32,512]{1,0:T(8,128)S(1)}, f32[32,512]{1,0:T(8,128)S(1)}, u32[]{:S(2)}, u32[]{:S(2)}) %collective-permute-start.30) | collective-permute-done | bytes 65568 | tf_op jit(solution)/shard_map/ppermute | solution.py:569
  196.9 1.0 collective-permute-done.31.refs_3_
  197.9 3.3 %left_factors.1 = (f32[128,512]{1,0:T(8,128)S(1)}, f32[40,512]{1,0:T(8,128)S(1)}, f32[8,120]{1,0:T(8,128)}, f32[8,480]{1,0:T(8,128)}, f32[8,1152]{1,0:T(8,128)S(...) custom-call(s32[1]{0:T(128)} %bitcast.group, f32[32,512]{1,0:T(8,128)S(1)} %add.65.refs_0_, ...), custom_call_target="tpu_custom_call" | custom-call | tf_op jit(solution)/shard_map/left_factors/pallas_call | solution.py:841
  201.3 1.2 collective-permute-start.33
  202.7 0.6 collective-permute-start.34
  203.5 1.9 collective-permute-done.33
  205.3 1.0 collective-permute-done.34
  206.4 0.6 collective-permute-start.35
  207.0 3.5 %collective-permute-done.35 = f32[8,1152]{1,0:T(8,128)S(1)} collective-permute-done((f32[8,1152]{1,0:T(8,128)S(1)}, f32[8,1152]{1,0:T(8,128)S(1)}, u32[]{:S(2)}, u32[]{:S(2)}) %collective-permute-start.35) | collective-permute-done | bytes 36896 | tf_op jit(solution)/shard_map/ppermute | solution.py:569
  210.4 3.9 %collective-permute-done.36 = f32[8,1152]{1,0:T(8,128)S(1)} collective-permute-done((f32[8,1152]{1,0:T(8,128)S(1)}, f32[8,1152]{1,0:T(8,128)S(1)}, u32[]{:S(2)}, u32[]{:S(2)}) %collective-permute-start.36) | collective-permute-done | bytes 36896 | tf_op jit(solution)/shard_map/ppermute | solution.py:569
  214.4 4.8 %collective-permute-done.37 = f32[8,1152]{1,0:T(8,128)S(1)} collective-permute-done((f32[8,1152]{1,0:T(8,128)S(1)}, f32[8,1152]{1,0:T(8,128)S(1)}, u32[]{:S(2)}, u32[]{:S(2)}) %collective-permute-start.37) | collective-permute-done | bytes 36896 | tf_op jit(solution)/shard_map/ppermute | solution.py:569
  219.3 0.8 collective-permute-start.39
  220.1 1.1 collective-permute-start.40
  221.1 2.4 %collective-permute-done.39.refs_2_ = f32[8,1152]{1,0:T(8,128)S(1)} collective-permute-done((f32[8,1152]{1,0:T(8,128)S(1)}, f32[8,1152]{1,0:T(8,128)S(1)}, u32[]{:S(2)}, u32[]{:S(2)}) %collective-permute-start.39) | collective-permute-done | bytes 36896 | tf_op jit(solution)/shard_map/ppermute | solution.py:569
  223.9 5.5 %finish.1 = (f32[1,1]{1,0:T(1,128)}, f32[1,1]{1,0:T(1,128)}, f32[1,1]{1,0:T(1,128)}, f32[8,3840]{1,0:T(8,128)}, f32[8,480]{1,0:T(8,128)}, /*index=5*/f32[120,384...) custom-call(s32[1]{0:T(128)} %bitcast.group, ...), custom_call_target="tpu_custom_call" | custom-call | tf_op jit(solution)/shard_map/finish/pallas_call | solution.py:870
  (168 shorter events, 3.6 us)
Async XLA Ops:
  2.5 11.9 %collective-permute-start = (bf16[120,1440]{1,0:T(8,128)(2,1)S(1)}, bf16[120,1440]{1,0:T(8,128)(2,1)}, u32[]{:S(2)}, u32[]{:S(2)}) collective-permute-start(bf16[120,1440]{1,0:T(8,128)(2,1)S(1)} %slice.15.refs_0_), channel_id=1, source_target_pairs={{0,2},{1,3},{2,0},{3,1},{4,6},{5,7},{6,4},{7,5},{8,10},{9,11},{10,... | collective-permute-start | bytes 1036808 | tf_op jit(solution)/shard_map/ppermute | solution.py:569
  6.8 6.9 %collective-permute-start.1 = (f32[8,128]{1,0:T(8,128)S(1)}, f32[8,128]{1,0:T(8,128)S(1)}, u32[]{:S(2)}, u32[]{:S(2)}) collective-permute-start(f32[8,128]{1,0:T(8,128)S(1)} %broadcast_in_dim.33), channel_id=1, source_target_pairs={{0,1},{1,0},{2,3},{3,2},{4,5},{5,4},{6,7},{7,6},{8,9},{9,8},{10,11... | collective-permute-start | bytes 12296 | tf_op jit(solution)/shard_map/ppermute | solution.py:569
  14.4 4.4 %collective-permute-start.2 = (bf16[120,1440]{1,0:T(8,128)(2,1)S(1)}, bf16[120,1440]{1,0:T(8,128)(2,1)S(1)}, u32[]{:S(2)}, u32[]{:S(2)}) collective-permute-start(bf16[120,1440]{1,0:T(8,128)(2,1)S(1)} %slice.15.refs_0_), channel_id=1, source_target_pairs={{0,1},{1,0},{2,3},{3,2},{4,5},{5,4},{6,7},{7,6},{8,9},{9,8},{10,11... | collective-permute-start | bytes 1036808 | tf_op jit(solution)/shard_map/ppermute | solution.py:569
  15.0 3.8 %collective-permute-start.3 = (bf16[120,1440]{1,0:T(8,128)(2,1)}, bf16[120,1440]{1,0:T(8,128)(2,1)S(1)}, u32[]{:S(2)}, u32[]{:S(2)}) collective-permute-start(bf16[120,1440]{1,0:T(8,128)(2,1)} %collective-permute-done.refs_2_), channel_id=1, source_target_pairs={{0,1},{1,0},{2,3},{3,2},{4,5},{5,4},{6,7},{7,6},{8,9},{9,8},{10,11... | collective-permute-start | bytes 1036808 | tf_op jit(solution)/shard_map/ppermute | solution.py:569
  15.1 32.0 %copy-start.47 = (bf16[120,2400]{1,0:T(8,128)(2,1)}, bf16[120,2400]{1,0:T(8,128)(2,1)S(1)}, u32[]{:S(2)}) copy-start(bf16[120,2400]{1,0:T(8,128)(2,1)S(1)} %pad_maximum_fusion.refs_0_) | copy-start | bytes 1728004
  15.1 3.7 %collective-permute-start.4 = (f32[8,128]{1,0:T(8,128)S(1)}, f32[8,128]{1,0:T(8,128)S(1)}, u32[]{:S(2)}, u32[]{:S(2)}) collective-permute-start(f32[8,128]{1,0:T(8,128)S(1)} %broadcast_add_fusion), channel_id=1, source_target_pairs={{0,2},{1,3},{2,0},{3,1},{4,6},{5,7},{6,4},{7,5},{8,10},{9,11},{10,... | collective-permute-start | bytes 12296 | tf_op jit(solution)/shard_map/ppermute | solution.py:569
  16.7 31.0 %copy-start.48 = (bf16[480,480]{1,0:T(8,128)(2,1)}, bf16[480,480]{1,0:T(8,128)(2,1)S(1)}, u32[]{:S(2)}) copy-start(bf16[480,480]{1,0:T(8,128)(2,1)S(1)} %bitcast_convert_fusion.refs_4_) | copy-start | bytes 1382404
  18.8 28.3 %collective-permute-start.7 = (bf16[120,2400]{1,0:T(8,128)(2,1)S(1)}, bf16[120,2400]{1,0:T(8,128)(2,1)S(1)}, u32[]{:S(2)}, u32[]{:S(2)}) collective-permute-start(bf16[120,2400]{1,0:T(8,128)(2,1)S(1)} %pad_maximum_fusion.refs_0_), channel_id=1, source_target_pairs={{0,2},{1,3},{2,0},{3,1},{4,6},{5,7},{6,4},{7,5},{8,10},{9,11},{10,... | collective-permute-start | bytes 1728008 | tf_op jit(solution)/shard_map/ppermute | solution.py:569
  20.3 26.8 %collective-permute-start.8 = (bf16[480,480]{1,0:T(8,128)(2,1)S(1)}, bf16[480,480]{1,0:T(8,128)(2,1)S(1)}, u32[]{:S(2)}, u32[]{:S(2)}) collective-permute-start(bf16[480,480]{1,0:T(8,128)(2,1)S(1)} %bitcast_convert_fusion.refs_4_), channel_id=1, source_target_pairs={{0,2},{1,3},{2,0},{3,1},{4,6},{5,7},{6,4},{7,5},{8,10},{9,11},{10,... | collective-permute-start | bytes 1382408 | tf_op jit(solution)/shard_map/ppermute | solution.py:569
  20.9 6.3 %collective-permute-start.5 = (f32[8,128]{1,0:T(8,128)S(1)}, f32[8,128]{1,0:T(8,128)S(1)}, u32[]{:S(2)}, u32[]{:S(2)}) collective-permute-start(f32[8,128]{1,0:T(8,128)S(1)} %add.55), channel_id=1, source_target_pairs={{0,4},{4,0},{8,12},{12,8},{16,20},{20,16},{24,28},{28,24},{1,5},{5... | collective-permute-start | bytes 12296 | tf_op jit(solution)/shard_map/ppermute | solution.py:569
  27.2 19.9 %collective-permute-start.6 = (f32[8,128]{1,0:T(8,128)S(1)}, f32[8,128]{1,0:T(8,128)S(1)}, u32[]{:S(2)}, u32[]{:S(2)}) collective-permute-start(f32[8,128]{1,0:T(8,128)S(1)} %add.56), channel_id=1, source_target_pairs={{0,8},{4,12},{8,0},{12,4},{16,24},{20,28},{24,16},{28,20},{1,9},{5... | collective-permute-start | bytes 12296 | tf_op jit(solution)/shard_map/ppermute | solution.py:569
  47.1 21.4 %copy-start.17 = (f32[240,1024]{1,0:T(8,128)}, f32[240,1024]{1,0:T(8,128)S(1)}, u32[]{:S(2)}) copy-start(f32[240,1024]{1,0:T(8,128)S(1)} %get-tuple-element.155.mixa_ref) | copy-start | bytes 2949124
  47.1 21.4 %copy-start.53 = (bf16[480,480]{1,0:T(8,128)(2,1)}, bf16[480,480]{1,0:T(8,128)(2,1)S(1)}, u32[]{:S(2)}) copy-start(bf16[480,480]{1,0:T(8,128)(2,1)S(1)} %collective-permute-done.8.refs_6_) | copy-start | bytes 1382404
  47.1 21.4 %copy-start.49 = (bf16[120,2400]{1,0:T(8,128)(2,1)}, bf16[120,2400]{1,0:T(8,128)(2,1)S(1)}, u32[]{:S(2)}) copy-start(bf16[120,2400]{1,0:T(8,128)(2,1)S(1)} %collective-permute-done.7.refs_2_) | copy-start | bytes 1728004
  47.2 23.5 %collective-permute-start.10 = (bf16[120,2400]{1,0:T(8,128)(2,1)S(1)}, bf16[120,2400]{1,0:T(8,128)(2,1)S(1)}, u32[]{:S(2)}, u32[]{:S(2)}) collective-permute-start(bf16[120,2400]{1,0:T(8,128)(2,1)S(1)} %pad_maximum_fusion.refs_0_), channel_id=1, source_target_pairs={{0,1},{1,0},{2,3},{3,2},{4,5},{5,4},{6,7},{7,6},{8,9},{9,8},{10,11... | collective-permute-start | bytes 1728008 | tf_op jit(solution)/shard_map/ppermute | solution.py:569
  47.2 23.5 %collective-permute-start.11 = (bf16[120,2400]{1,0:T(8,128)(2,1)S(1)}, bf16[120,2400]{1,0:T(8,128)(2,1)S(1)}, u32[]{:S(2)}, u32[]{:S(2)}) collective-permute-start(bf16[120,2400]{1,0:T(8,128)(2,1)S(1)} %collective-permute-done.7.refs_2_), channel_id=1, source_target_pairs={{0,1},{1,0},{2,3},{3,2},{4,5},{5,4},{6,7},{7,6},{8,9},{9,8},{10,11... | collective-permute-start | bytes 1728008 | tf_op jit(solution)/shard_map/ppermute | solution.py:569
  47.7 22.9 %collective-permute-start.12 = (bf16[480,480]{1,0:T(8,128)(2,1)S(1)}, bf16[480,480]{1,0:T(8,128)(2,1)S(1)}, u32[]{:S(2)}, u32[]{:S(2)}) collective-permute-start(bf16[480,480]{1,0:T(8,128)(2,1)S(1)} %bitcast_convert_fusion.refs_4_), channel_id=1, source_target_pairs={{0,1},{1,0},{2,3},{3,2},{4,5},{5,4},{6,7},{7,6},{8,9},{9,8},{10,11... | collective-permute-start | bytes 1382408 | tf_op jit(solution)/shard_map/ppermute | solution.py:569
  47.8 22.9 %collective-permute-start.13 = (bf16[480,480]{1,0:T(8,128)(2,1)S(1)}, bf16[480,480]{1,0:T(8,128)(2,1)S(1)}, u32[]{:S(2)}, u32[]{:S(2)}) collective-permute-start(bf16[480,480]{1,0:T(8,128)(2,1)S(1)} %collective-permute-done.8.refs_6_), channel_id=1, source_target_pairs={{0,1},{1,0},{2,3},{3,2},{4,5},{5,4},{6,7},{7,6},{8,9},{9,8},{10,11... | collective-permute-start | bytes 1382408 | tf_op jit(solution)/shard_map/ppermute | solution.py:569
  48.2 21.8 %collective-permute-start.9 = (f32[8,128]{1,0:T(8,128)S(1)}, f32[8,128]{1,0:T(8,128)S(1)}, u32[]{:S(2)}, u32[]{:S(2)}) collective-permute-start(f32[8,128]{1,0:T(8,128)S(1)} %add.57), channel_id=1, source_target_pairs={{0,16},{4,20},{8,24},{12,28},{16,0},{20,4},{24,8},{28,12},{1,17},{... | collective-permute-start | bytes 12296 | tf_op jit(solution)/shard_map/ppermute | solution.py:569
  106.1 3.4 %collective-permute-start.14 = (bf16[480,480]{1,0:T(8,128)(2,1)}, bf16[480,480]{1,0:T(8,128)(2,1)S(1)}, u32[]{:S(2)}, u32[]{:S(2)}) collective-permute-start(bf16[480,480]{1,0:T(8,128)(2,1)} %get-tuple-element.178.refs_13_), channel_id=1, source_target_pairs={{0,1},{1,0},{2,3},{3,2},{4,5},{5,4},{6,7},{7,6},{8,9},{9,8},{10,11... | collective-permute-start | bytes 1382408 | tf_op jit(solution)/shard_map/ppermute | solution.py:569
  106.2 51.4 %collective-permute-start.17 = (bf16[120,2400]{1,0:T(8,128)(2,1)}, bf16[120,2400]{1,0:T(8,128)(2,1)S(1)}, u32[]{:S(2)}, u32[]{:S(2)}) collective-permute-start(bf16[120,2400]{1,0:T(8,128)(2,1)} %get-tuple-element.182.refs_9_), channel_id=1, source_target_pairs={{0,1},{1,0},{2,3},{3,2},{4,5},{5,4},{6,7},{7,6},{8,9},{9,8},{10,11... | collective-permute-start | bytes 1728008 | tf_op jit(solution)/shard_map/ppermute | solution.py:569
  106.7 50.9 %collective-permute-start.18 = (bf16[120,2400]{1,0:T(8,128)(2,1)}, bf16[120,2400]{1,0:T(8,128)(2,1)S(1)}, u32[]{:S(2)}, u32[]{:S(2)}) collective-permute-start(bf16[120,2400]{1,0:T(8,128)(2,1)} %get-tuple-element.183.refs_10_), channel_id=1, source_target_pairs={{0,2},{1,3},{2,0},{3,1},{4,6},{5,7},{6,4},{7,5},{8,10},{9,11},{10,... | collective-permute-start | bytes 1728008 | tf_op jit(solution)/shard_map/ppermute | solution.py:569
  108.1 49.4 %collective-permute-start.19 = (bf16[120,2400]{1,0:T(8,128)(2,1)}, bf16[120,2400]{1,0:T(8,128)(2,1)S(1)}, u32[]{:S(2)}, u32[]{:S(2)}) collective-permute-start(bf16[120,2400]{1,0:T(8,128)(2,1)} %get-tuple-element.184.refs_11_), channel_id=1, source_target_pairs={{0,3},{1,2},{2,1},{3,0},{4,7},{5,6},{6,5},{7,4},{8,11},{9,10},{10,... | collective-permute-start | bytes 1728008 | tf_op jit(solution)/shard_map/ppermute | solution.py:569
  108.1 49.4 %collective-permute-start.15 = (bf16[480,480]{1,0:T(8,128)(2,1)}, bf16[480,480]{1,0:T(8,128)(2,1)S(1)}, u32[]{:S(2)}, u32[]{:S(2)}) collective-permute-start(bf16[480,480]{1,0:T(8,128)(2,1)} %get-tuple-element.179.refs_14_), channel_id=1, source_target_pairs={{0,2},{1,3},{2,0},{3,1},{4,6},{5,7},{6,4},{7,5},{8,10},{9,11},{10,... | collective-permute-start | bytes 1382408 | tf_op jit(solution)/shard_map/ppermute | solution.py:569
  109.5 48.0 %collective-permute-start.16 = (bf16[480,480]{1,0:T(8,128)(2,1)}, bf16[480,480]{1,0:T(8,128)(2,1)S(1)}, u32[]{:S(2)}, u32[]{:S(2)}) collective-permute-start(bf16[480,480]{1,0:T(8,128)(2,1)} %get-tuple-element.180.refs_15_), channel_id=1, source_target_pairs={{0,3},{1,2},{2,1},{3,0},{4,7},{5,6},{6,5},{7,4},{8,11},{9,10},{10,... | collective-permute-start | bytes 1382408 | tf_op jit(solution)/shard_map/ppermute | solution.py:569
  111.5 46.1 %copy-start.3 = (f32[1024,480]{1,0:T(8,128)S(1)}, f32[1024,480]{1,0:T(8,128)}, u32[]{:S(2)}) copy-start(f32[1024,480]{1,0:T(8,128)} %copy-done.2) | copy-start | bytes 5898244
  111.5 46.1 %copy-start.8 = (f32[1024,480]{1,0:T(8,128)S(1)}, f32[1024,480]{1,0:T(8,128)}, u32[]{:S(2)}) copy-start(f32[1024,480]{1,0:T(8,128)} %get-tuple-element.190.dx_ref) | copy-start | bytes 5898244
  111.5 46.1 %copy-start.13 = (f32[1,3840,8]{1,2,0:T(8,128)S(1)}, f32[1,3840,8]{1,2,0:T(8,128)}, u32[]{:S(2)}) copy-start(f32[1,3840,8]{1,2,0:T(8,128)} %param.30) | copy-start | bytes 368644
  111.5 46.1 %copy-start.15 = (bf16[496,1024]{1,0:T(8,128)(2,1)S(1)}, bf16[496,1024]{1,0:T(8,128)(2,1)}, u32[]{:S(2)}) copy-start(bf16[496,1024]{1,0:T(8,128)(2,1)} %copy-done.14) | copy-start | bytes 3047428
  111.5 46.1 %copy-start.20 = (f32[1,6240]{1,0:T(1,128)S(1)}, f32[1,6240]{1,0:T(1,128)}, u32[]{:S(2)}) copy-start(f32[1,6240]{1,0:T(1,128)} %refs_16_.1) | copy-start | bytes 74884
  111.5 46.1 %copy-start.32 = (f32[56,512]{1,0:T(8,128)S(1)}, f32[56,512]{1,0:T(8,128)}, u32[]{:S(2)}) copy-start(f32[56,512]{1,0:T(8,128)} %get-tuple-element.193.e_ref) | copy-start | bytes 344068
  111.5 46.1 %copy-start.35 = (f32[40,512]{1,0:T(8,128)S(1)}, f32[40,512]{1,0:T(8,128)}, u32[]{:S(2)}) copy-start(f32[40,512]{1,0:T(8,128)} %get-tuple-element.191.s_ref) | copy-start | bytes 245764
  167.5 2.7 %collective-permute-start.25 = (bf16[120,1440]{1,0:T(8,128)(2,1)S(1)}, bf16[120,1440]{1,0:T(8,128)(2,1)S(1)}, u32[]{:S(2)}, u32[]{:S(2)}) collective-permute-start(bf16[120,1440]{1,0:T(8,128)(2,1)S(1)} %get-tuple-element.209.refs_7_), channel_id=1, source_target_pairs={{0,1},{1,0},{2,3},{3,2},{4,5},{5,4},{6,7},{7,6},{8,9},{9,8},{10,11... | collective-permute-start | bytes 1036808 | tf_op jit(solution)/shard_map/ppermute | solution.py:569
  167.7 4.4 %collective-permute-start.20 = (f32[32,512]{1,0:T(8,128)S(1)}, f32[32,512]{1,0:T(8,128)S(1)}, u32[]{:S(2)}, u32[]{:S(2)}) collective-permute-start(f32[32,512]{1,0:T(8,128)S(1)} %get-tuple-element.195), channel_id=1, source_target_pairs={{0,1},{1,0},{2,3},{3,2},{4,5},{5,4},{6,7},{7,6},{8,9},{9,8},{10,11... | collective-permute-start | bytes 196616 | tf_op jit(solution)/shard_map/ppermute | solution.py:569
  168.1 4.3 %collective-permute-start.21 = (f32[32,512]{1,0:T(8,128)S(1)}, f32[32,512]{1,0:T(8,128)S(1)}, u32[]{:S(2)}, u32[]{:S(2)}) collective-permute-start(f32[32,512]{1,0:T(8,128)S(1)} %get-tuple-element.196), channel_id=1, source_target_pairs={{0,2},{1,3},{2,0},{3,1},{4,6},{5,7},{6,4},{7,5},{8,10},{9,11},{10,... | collective-permute-start | bytes 196616 | tf_op jit(solution)/shard_map/ppermute | solution.py:569
  169.5 4.4 %collective-permute-start.22 = (f32[32,512]{1,0:T(8,128)S(1)}, f32[32,512]{1,0:T(8,128)S(1)}, u32[]{:S(2)}, u32[]{:S(2)}) collective-permute-start(f32[32,512]{1,0:T(8,128)S(1)} %get-tuple-element.197), channel_id=1, source_target_pairs={{0,3},{1,2},{2,1},{3,0},{4,7},{5,6},{6,5},{7,4},{8,11},{9,10},{10,... | collective-permute-start | bytes 196616 | tf_op jit(solution)/shard_map/ppermute | solution.py:569
  169.6 8.7 %collective-permute-start.24 = (bf16[120,1440]{1,0:T(8,128)(2,1)S(1)}, bf16[120,1440]{1,0:T(8,128)(2,1)S(1)}, u32[]{:S(2)}, u32[]{:S(2)}) collective-permute-start(bf16[120,1440]{1,0:T(8,128)(2,1)S(1)} %get-tuple-element.207.refs_5_), channel_id=1, source_target_pairs={{0,1},{1,0},{2,3},{3,2},{4,5},{5,4},{6,7},{7,6},{8,9},{9,8},{10,11... | collective-permute-start | bytes 1036808 | tf_op jit(solution)/shard_map/ppermute | solution.py:569
  170.3 11.5 %collective-permute-start.26 = (bf16[120,1440]{1,0:T(8,128)(2,1)S(1)}, bf16[120,1440]{1,0:T(8,128)(2,1)S(1)}, u32[]{:S(2)}, u32[]{:S(2)}) collective-permute-start(bf16[120,1440]{1,0:T(8,128)(2,1)S(1)} %add_convert_fusion), channel_id=1, source_target_pairs={{0,2},{1,3},{2,0},{3,1},{4,6},{5,7},{6,4},{7,5},{8,10},{9,11},{10,... | collective-permute-start | bytes 1036808 | tf_op jit(solution)/shard_map/ppermute | solution.py:569
  173.9 4.3 %collective-permute-start.23 = (f32[32,512]{1,0:T(8,128)S(1)}, f32[32,512]{1,0:T(8,128)S(1)}, u32[]{:S(2)}, u32[]{:S(2)}) collective-permute-start(f32[32,512]{1,0:T(8,128)S(1)} %add_add_fusion), channel_id=1, source_target_pairs={{0,4},{4,0},{8,12},{12,8},{16,20},{20,16},{24,28},{28,24},{1,5},{5... | collective-permute-start | bytes 196616 | tf_op jit(solution)/shard_map/ppermute | solution.py:569
  181.9 4.3 %collective-permute-start.27 = (f32[32,512]{1,0:T(8,128)S(1)}, f32[32,512]{1,0:T(8,128)S(1)}, u32[]{:S(2)}, u32[]{:S(2)}) collective-permute-start(f32[32,512]{1,0:T(8,128)S(1)} %add.63), channel_id=1, source_target_pairs={{0,8},{4,12},{8,0},{12,4},{16,24},{20,28},{24,16},{28,20},{1,9},{5... | collective-permute-start | bytes 196616 | tf_op jit(solution)/shard_map/ppermute | solution.py:569
  186.2 5.8 %collective-permute-start.28 = (f32[32,512]{1,0:T(8,128)S(1)}, f32[32,512]{1,0:T(8,128)S(1)}, u32[]{:S(2)}, u32[]{:S(2)}) collective-permute-start(f32[32,512]{1,0:T(8,128)S(1)} %add.64), channel_id=1, source_target_pairs={{0,16},{4,20},{8,24},{12,28},{16,0},{20,4},{24,8},{28,12},{1,17},{... | collective-permute-start | bytes 196616 | tf_op jit(solution)/shard_map/ppermute | solution.py:569
  192.1 1.9 collective-permute-start.29
  192.1 4.7 %collective-permute-start.30 = (f32[32,512]{1,0:T(8,128)S(1)}, f32[32,512]{1,0:T(8,128)S(1)}, u32[]{:S(2)}, u32[]{:S(2)}) collective-permute-start(f32[32,512]{1,0:T(8,128)S(1)} %add.65.refs_0_), channel_id=1, source_target_pairs={{0,2},{1,3},{2,0},{3,1},{4,6},{5,7},{6,4},{7,5},{8,10},{9,11},{10,... | collective-permute-start | bytes 196616 | tf_op jit(solution)/shard_map/ppermute | solution.py:569
  193.5 4.3 %collective-permute-start.31 = (f32[32,512]{1,0:T(8,128)S(1)}, f32[32,512]{1,0:T(8,128)S(1)}, u32[]{:S(2)}, u32[]{:S(2)}) collective-permute-start(f32[32,512]{1,0:T(8,128)S(1)} %add.65.refs_0_), channel_id=1, source_target_pairs={{0,3},{1,2},{2,1},{3,0},{4,7},{5,6},{6,5},{7,4},{8,11},{9,10},{10,... | collective-permute-start | bytes 196616 | tf_op jit(solution)/shard_map/ppermute | solution.py:569
  197.9 26.0 %copy-start.10 = (f32[1,120,3840]{2,1,0:T(8,128)S(1)}, f32[1,120,3840]{2,1,0:T(8,128)}, u32[]{:S(2)}) copy-start(f32[1,120,3840]{2,1,0:T(8,128)} %param.26) | copy-start | bytes 5529604
  201.2 2.2 collective-permute-start.32
  201.3 4.0 %collective-permute-start.33 = (f32[8,1152]{1,0:T(8,128)S(1)}, f32[8,1152]{1,0:T(8,128)S(1)}, u32[]{:S(2)}, u32[]{:S(2)}) collective-permute-start(f32[8,1152]{1,0:T(8,128)S(1)} %get-tuple-element.218), channel_id=1, source_target_pairs={{0,2},{1,3},{2,0},{3,1},{4,6},{5,7},{6,4},{7,5},{8,10},{9,11},{10,... | collective-permute-start | bytes 110600 | tf_op jit(solution)/shard_map/ppermute | solution.py:569
  202.6 21.3 %copy-start.16 = (f32[1,480,480]{2,1,0:T(8,128)S(1)}, f32[1,480,480]{2,1,0:T(8,128)}, u32[]{:S(2)}) copy-start(f32[1,480,480]{2,1,0:T(8,128)} %param.27) | copy-start | bytes 2764804
  202.6 21.3 %copy-start.29 = (f32[481,33]{0,1:T(8,128)S(1)}, f32[481,33]{0,1:T(8,128)}, u32[]{:S(2)}) copy-start(f32[481,33]{0,1:T(8,128)} %param.38) | copy-start | bytes 190480
  202.6 21.3 %copy-start.31 = (f32[33,480]{1,0:T(8,128)S(1)}, f32[33,480]{1,0:T(8,128)}, u32[]{:S(2)}) copy-start(f32[33,480]{1,0:T(8,128)} %refs_20_.1) | copy-start | bytes 190084
  202.6 21.3 %copy-start.33 = (f32[33,480]{1,0:T(8,128)S(1)}, f32[33,480]{1,0:T(8,128)}, u32[]{:S(2)}) copy-start(f32[33,480]{1,0:T(8,128)} %refs_21_.1) | copy-start | bytes 190084
  202.6 21.3 %copy-start.34 = (f32[481,33]{0,1:T(8,128)S(1)}, f32[481,33]{0,1:T(8,128)}, u32[]{:S(2)}) copy-start(f32[481,33]{0,1:T(8,128)} %param.39) | copy-start | bytes 190480
  202.6 21.3 %copy-start.39 = (f32[8,128]{1,0:T(8,128)S(1)}, f32[8,128]{1,0:T(8,128)}, u32[]{:S(2)}) copy-start(f32[8,128]{1,0:T(8,128)} %add.58.count_ref.refs_15_) | copy-start | bytes 12292
  202.6 21.3 %copy-start.40 = (f32[1,6240]{1,0:T(1,128)S(1)}, f32[1,6240]{1,0:T(1,128)}, u32[]{:S(2)}) copy-start(f32[1,6240]{1,0:T(1,128)} %refs_17_.1) | copy-start | bytes 74884
  202.6 21.3 %copy-start.42 = (f32[8,480]{1,0:T(8,128)S(1)}, f32[8,480]{1,0:T(8,128)}, u32[]{:S(2)}) copy-start(f32[8,480]{1,0:T(8,128)} %get-tuple-element.230.refs_7_) | copy-start | bytes 46084
  202.6 21.3 %copy-start.43 = (f32[2,480]{1,0:T(2,128)S(1)}, f32[2,480]{1,0:T(2,128)}, u32[]{:S(2)}) copy-start(f32[2,480]{1,0:T(2,128)} %refs_18_.1) | copy-start | bytes 11524
  202.6 21.3 %copy-start.44 = (f32[2,480]{1,0:T(2,128)S(1)}, f32[2,480]{1,0:T(2,128)}, u32[]{:S(2)}) copy-start(f32[2,480]{1,0:T(2,128)} %refs_19_.1) | copy-start | bytes 11524
  202.7 3.7 %collective-permute-start.34 = (f32[8,1152]{1,0:T(8,128)S(1)}, f32[8,1152]{1,0:T(8,128)S(1)}, u32[]{:S(2)}, u32[]{:S(2)}) collective-permute-start(f32[8,1152]{1,0:T(8,128)S(1)} %get-tuple-element.219), channel_id=1, source_target_pairs={{0,3},{1,2},{2,1},{3,0},{4,7},{5,6},{6,5},{7,4},{8,11},{9,10},{10,... | collective-permute-start | bytes 110600 | tf_op jit(solution)/shard_map/ppermute | solution.py:569
  206.4 4.0 %collective-permute-start.35 = (f32[8,1152]{1,0:T(8,128)S(1)}, f32[8,1152]{1,0:T(8,128)S(1)}, u32[]{:S(2)}, u32[]{:S(2)}) collective-permute-start(f32[8,1152]{1,0:T(8,128)S(1)} %add_add_fusion.1), channel_id=1, source_target_pairs={{0,4},{4,0},{8,12},{12,8},{16,20},{20,16},{24,28},{28,24},{1,5},{5... | collective-permute-start | bytes 110600 | tf_op jit(solution)/shard_map/ppermute | solution.py:569
  210.4 4.0 %collective-permute-start.36 = (f32[8,1152]{1,0:T(8,128)S(1)}, f32[8,1152]{1,0:T(8,128)S(1)}, u32[]{:S(2)}, u32[]{:S(2)}) collective-permute-start(f32[8,1152]{1,0:T(8,128)S(1)} %add.69), channel_id=1, source_target_pairs={{0,8},{4,12},{8,0},{12,4},{16,24},{20,28},{24,16},{28,20},{1,9},{5... | collective-permute-start | bytes 110600 | tf_op jit(solution)/shard_map/ppermute | solution.py:569
  214.4 4.9 %collective-permute-start.37 = (f32[8,1152]{1,0:T(8,128)S(1)}, f32[8,1152]{1,0:T(8,128)S(1)}, u32[]{:S(2)}, u32[]{:S(2)}) collective-permute-start(f32[8,1152]{1,0:T(8,128)S(1)} %add.70), channel_id=1, source_target_pairs={{0,16},{4,20},{8,24},{12,28},{16,0},{20,4},{24,8},{28,12},{1,17},{... | collective-permute-start | bytes 110600 | tf_op jit(solution)/shard_map/ppermute | solution.py:569
  219.3 1.9 collective-permute-start.38
  219.3 4.3 %collective-permute-start.39 = (f32[8,1152]{1,0:T(8,128)S(1)}, f32[8,1152]{1,0:T(8,128)S(1)}, u32[]{:S(2)}, u32[]{:S(2)}) collective-permute-start(f32[8,1152]{1,0:T(8,128)S(1)} %add.71.refs_0_), channel_id=1, source_target_pairs={{0,2},{1,3},{2,0},{3,1},{4,6},{5,7},{6,4},{7,5},{8,10},{9,11},{10,... | collective-permute-start | bytes 110600 | tf_op jit(solution)/shard_map/ppermute | solution.py:569
  220.1 3.8 %collective-permute-start.40 = (f32[8,1152]{1,0:T(8,128)S(1)}, f32[8,1152]{1,0:T(8,128)S(1)}, u32[]{:S(2)}, u32[]{:S(2)}) collective-permute-start(f32[8,1152]{1,0:T(8,128)S(1)} %add.71.refs_0_), channel_id=1, source_target_pairs={{0,3},{1,2},{2,1},{3,0},{4,7},{5,6},{6,5},{7,4},{8,11},{9,10},{10,... | collective-permute-start | bytes 110600 | tf_op jit(solution)/shard_map/ppermute | solution.py:569
  (35 other events, 309.8 us)
where the time goes:
time: 230 us
  Pallas kernels  143 us (62%)
  waiting for transfers between devices  41.6 us (18%)
  starting transfers between devices  30.2 us (13%)
  local copies, waits for them, and re-layouts  9.11 us (4%)
  other arithmetic  3.93 us (2%)
    pallas_call x1, Pallas kernels, shards(): pl.pallas_call(attend_back_kernel, grid=(HEADS // pair,), in_specs=[pl.Bl...  46 us
    ppermute x41, waiting for transfers between devices, swap(): return lax.ppermute(value, axis, [(i, i ^ bit) for i in range(size)])  41.6 us
    pallas_call x2, Pallas kernels, shards(): pl.pallas_call(attend_kernel, grid=(half,), in_specs=[one, one, one] + [p...  35.3 us
    pallas_call x1, Pallas kernels, shards(): call(partial(middle_kernel, members), 'feed_and_loss', (length // step_mi...  33.7 us
    ppermute x41, starting transfers between devices, swap(): return lax.ppermute(value, axis, [(i, i ^ bit) for i in range(size)])  30.2 us
    pallas_call x1, Pallas kernels, shards(): call(partial(input_kernel, members), 'input_grads', (steps,), [cols, act,...  9.85 us
    unnamed x114, local copies, waits for them, and re-layouts  7.68 us
    pallas_call x1, Pallas kernels, shards(): call(partial(finish_kernel, members, replicas), 'finish', (1,), [whole(it...  5.5 us
  transfers between devices with their start and end apart: 41, of which 16 were waited for; matrix products, arithmetic and copies ran while one was open for 2% of the time, Pallas kernels for 40%

commit v1 on v0

--- a/solution.py
+++ b/solution.py
@@ -597,8 +597,11 @@
     total = got[0]
     for piece in got[1:]:
         total = total + piece
-    for turn, bit in enumerate(bits_of("rep")):
-        total = total + beside(turn + 1, swap(total, "rep", bit))
+    first, *bits = bits_of("rep")
+    for turn, pair in enumerate([[first]] + [bits[at : at + 2] for at in range(0, len(bits), 2)]):
+        moves = pair + [sum(pair)] * (len(pair) - 1)
+        for piece in beside(turn + 1, [swap(total, "rep", move) for move in moves]):
+            total = total + piece
     got = [total] + [swap(total, "grp", place) for place in range(1, len(pieces))]
     return beside(-1, got), results
 

time: 230 us -> 228 us (level)
  waiting for transfers between devices: 41.6 us -> 31.5 us
  starting transfers between devices: 30.2 us -> 38.2 us
    ppermute x41 -> x43, waiting for transfers between devices: 41.6 us -> 31.5 us  [swap(): return lax.ppermute(value, axis, [(i, i ^ bit) for i in range(size)])]
    ppermute x41 -> x43, starting transfers between devices: 30.2 us -> 38.2 us  [swap(): return lax.ppermute(value, axis, [(i, i ^ bit) for i in range(size)])]
    unnamed x114 -> x112, local copies, waits for them, and re-layouts: 7.68 us -> 7.66 us
  transfers between devices with their start and end apart: 41 -> 43, of which waited for: 16 -> 15; matrix products, arithmetic and copies ran while one was open for 2% -> 2% of each run, Pallas kernels for 40% -> 40%
where the time goes in v1:
time: 228 us
  Pallas kernels  143 us (63%)
  starting transfers between devices  38.2 us (17%)
  waiting for transfers between devices  31.5 us (14%)
  local copies, waits for them, and re-layouts  9.09 us (4%)
  other arithmetic  3.93 us (2%)
    pallas_call x1, Pallas kernels, shards(): pl.pallas_call(attend_back_kernel, grid=(HEADS // pair,), in_specs=[pl.Bl...  45.9 us
    ppermute x43, starting transfers between devices, swap(): return lax.ppermute(value, axis, [(i, i ^ bit) for i in range(size)])  38.2 us
    pallas_call x2, Pallas kernels, shards(): pl.pallas_call(attend_kernel, grid=(half,), in_specs=[one, one, one] + [p...  35.3 us
    pallas_call x1, Pallas kernels, shards(): call(partial(middle_kernel, members), 'feed_and_loss', (length // step_mi...  33.6 us
    ppermute x43, waiting for transfers between devices, swap(): return lax.ppermute(value, axis, [(i, i ^ bit) for i in range(size)])  31.5 us
    pallas_call x1, Pallas kernels, shards(): call(partial(input_kernel, members), 'input_grads', (steps,), [cols, act,...  9.86 us
    unnamed x112, local copies, waits for them, and re-layouts  7.66 us
    pallas_call x1, Pallas kernels, shards(): call(partial(finish_kernel, members, replicas), 'finish', (1,), [whole(it...  5.53 us
  transfers between devices with their start and end apart: 43, of which 15 were waited for; matrix products, arithmetic and copies ran while one was open for 2% of the time, Pallas kernels for 40%

profile of v1, /device:TPU:0, one launch (start us, length us, event | category | flops | bytes accessed | tf_op | source)
XLA Modules:
  0.0 227.6 jit_solution(3414103817137611542)
XLA Ops:
  0.7 1.8 bitcast_convert_fusion.1
  2.5 3.0 %collective-permute-start = (bf16[120,1440]{1,0:T(8,128)(2,1)S(1)}, bf16[120,1440]{1,0:T(8,128)(2,1)}, u32[]{:S(2)}, u32[]{:S(2)}) collective-permute-start(bf16[120,1440]{1,0:T(8,128)(2,1)S(1)} %slice.15.refs_0_), channel_id=1, source_target_pairs={{0,2},{1,3},{2,0},{3,1},{4,6},{5,7},{6,4},{7,5},{8,10},{9,11},{10,... | collective-permute-start | bytes 1036808 | tf_op jit(solution)/shard_map/ppermute | solution.py:569
  5.6 0.6 convert_reduce_fusion
  6.2 0.6 broadcast_in_dim.33
  6.9 0.8 slice.17
  7.7 2.2 embed.1
  9.9 1.3 copy-done.2
  11.2 1.0 copy-done.14
  12.2 1.5 error_sketch.1.serr_ref
  13.7 0.7 broadcast_add_fusion
  14.4 0.6 collective-permute-start.2
  15.1 1.5 collective-permute-start.4
  16.7 2.1 collective-permute-done.4
  18.8 1.5 collective-permute-start.7
  20.3 0.6 collective-permute-start.8
  20.9 1.5 collective-permute-start.5
  22.4 4.8 %project.1 = (bf16[20,32,1024]{2,1,0:T(8,128)(2,1)S(1)}, bf16[20,32,1024]{2,1,0:T(8,128)(2,1)S(1)}, bf16[20,32,1024]{2,1,0:T(8,128)(2,1)S(1)}) custom-call(s32[1]{0:T(128)} %bitcast.group, bf16[1024,480]{1,0:T(8,128)(2,1)S(1)} %get-tuple-element.140.h_ref, bf16[120,1440]{1,0:T(8,128)(2,1)S(1)} %slice.15.refs_0_, ...), custom_call_target="tpu_custom_call" | custom-call | tf_op jit(solution)/shard_map/project/pallas_call | solution.py:717
  27.2 1.6 collective-permute-start.6
  28.9 17.7 %attend.2 = (f32[240,1024]{1,0:T(8,128)S(1)}, f32[10,1,1024]{2,1,0:T(1,128)S(1)}, bf16[20,1024,1024]{2,1,0:T(8,128)(2,1)}) custom-call(bf16[20,32,1024]{2,1,0:T(8,128)(2,1)S(1)} %get-tuple-element.188.q_ref, bf16[20,32,1024]{2,1,0:T(8,128)(2,1)S(1)} %get-tuple-element.151.k_ref, bf16[20,32,1024]{2,1,0:T(8,128)(2,1)S(1)} %get-tuple-element.152.v_ref), custom_call_target="tpu_custom_call" | custom-call | tf_op jit(solution)/shard_map/attend/pallas_call | solution.py:732
  46.5 0.6 copy-done.36
  48.3 2.6 %collective-permute-start.9 = (f32[8,128]{1,0:T(8,128)S(1)}, f32[8,128]{1,0:T(8,128)S(1)}, u32[]{:S(2)}, u32[]{:S(2)}) collective-permute-start(f32[8,128]{1,0:T(8,128)S(1)} %add.63), channel_id=1, source_target_pairs={{0,16},{4,20},{8,24},{12,28},{16,0},{20,4},{24,8},{28,12},{1,17},{... | collective-permute-start | bytes 12296 | tf_op jit(solution)/shard_map/ppermute | solution.py:569
  50.9 17.6 %attend.3 = (f32[240,1024]{1,0:T(8,128)S(1)}, f32[10,1,1024]{2,1,0:T(1,128)S(1)}, bf16[20,1024,1024]{2,1,0:T(8,128)(2,1)}) custom-call(bf16[20,32,1024]{2,1,0:T(8,128)(2,1)S(1)} %get-tuple-element.188.q_ref, bf16[20,32,1024]{2,1,0:T(8,128)(2,1)S(1)} %get-tuple-element.151.k_ref, ...), custom_call_target="tpu_custom_call", output_to_operand_aliasing={{2}: (3, {})} | custom-call | tf_op jit(solution)/shard_map/attend/pallas_call | solution.py:732
  68.5 0.9 copy-done.18
  69.5 0.6 copy-done.37
  70.1 0.6 add.64.count_ref.refs_15_
  70.7 0.9 copy-done.49
  71.6 0.8 copy-done.50
  72.4 33.6 %feed_and_loss.1 = (bf16[20,32,1024]{2,1,0:T(8,128)(2,1)}, f32[1024,480]{1,0:T(8,128)}, f32[40,512]{1,0:T(8,128)}, f32[56,512]{1,0:T(8,128)}, bf16[120,2400]{1,0...) custom-call(s32[1]{0:T(128)} %bitcast.group, ...), custom_call_target="tpu_custom_call" | custom-call | tf_op jit(solution)/shard_map/feed_and_loss/pallas_call | solution.py:760
  106.7 1.5 collective-permute-start.18
  108.1 1.4 collective-permute-start.15
  109.6 0.6 collective-permute-start.16
  110.2 1.3 copy-done.11
  111.5 45.9 %attend_back.1.da_ref = bf16[3,480,1024]{2,1,0:T(8,128)(2,1)S(1)} custom-call(bf16[20,1024,1024]{2,1,0:T(8,128)(2,1)} %get-tuple-element.187.p_ref, bf16[20,32,1024]{2,1,0:T(8,128)(2,1)S(1)} %get-tuple-element.188.q_ref, bf16[20,32,1024]{2,1,0:T(8,128)(2,1)S(1)} %get-tuple-element.151.k_ref, bf16[20,32,1024]{2,1,0:T(8,128)(2,1)S(1)} %get-tuple-element.152.v_ref, ...), custom_call_target="tpu_custom_call" | custom-call | tf_op jit(solution)/shard_map/attend_back/pallas_call | solution.py:795
  157.6 9.9 %input_grads.1 = (bf16[120,1440]{1,0:T(8,128)(2,1)S(1)}, bf16[120,1440]{1,0:T(8,128)(2,1)S(1)}, bf16[120,1440]{1,0:T(8,128)(2,1)S(1)}, bf16[120,1440]{1,0:T(8,12...) custom-call(s32[1]{0:T(128)} %bitcast.group, ...), custom_call_target="tpu_custom_call" | custom-call | tf_op jit(solution)/shard_map/input_grads/pallas_call | solution.py:812
  168.0 1.5 collective-permute-start.21
  169.6 0.6 collective-permute-start.24
  170.3 1.6 collective-permute-start.26
  172.3 1.6 collective-permute-done.22
  173.9 0.5 collective-permute-start.23
  174.4 3.8 %collective-permute-done.23 = f32[32,512]{1,0:T(8,128)S(1)} collective-permute-done((f32[32,512]{1,0:T(8,128)S(1)}, f32[32,512]{1,0:T(8,128)S(1)}, u32[]{:S(2)}, u32[]{:S(2)}) %collective-permute-start.23) | collective-permute-done | bytes 65568 | tf_op jit(solution)/shard_map/ppermute | solution.py:569
  178.3 3.5 %collective-permute-done.26.refs_2_ = bf16[120,1440]{1,0:T(8,128)(2,1)S(1)} collective-permute-done((bf16[120,1440]{1,0:T(8,128)(2,1)S(1)}, bf16[120,1440]{1,0:T(8,128)(2,1)S(1)}, u32[]{:S(2)}, u32[]{:S(2)}) %collective-permute-start.26) | collective-permute-done | bytes 345632 | tf_op jit(solution)/shard_map/ppermute | solution.py:569
  181.9 0.5 collective-permute-start.27
  182.7 3.7 %collective-permute-start.29 = (f32[32,512]{1,0:T(8,128)S(1)}, f32[32,512]{1,0:T(8,128)S(1)}, u32[]{:S(2)}, u32[]{:S(2)}) collective-permute-start(f32[32,512]{1,0:T(8,128)S(1)} %add.69), channel_id=1, source_target_pairs={{0,24},{4,28},{8,16},{12,20},{16,8},{20,12},{24,0},{28,4},{1,25},{... | collective-permute-start | bytes 196616 | tf_op jit(solution)/shard_map/ppermute | solution.py:569
  186.3 0.6 merge_rest.1.refs_13_
  186.9 3.6 %collective-permute-done.28 = f32[32,512]{1,0:T(8,128)S(1)} collective-permute-done((f32[32,512]{1,0:T(8,128)S(1)}, f32[32,512]{1,0:T(8,128)S(1)}, u32[]{:S(2)}, u32[]{:S(2)}) %collective-permute-start.28) | collective-permute-done | bytes 65568 | tf_op jit(solution)/shard_map/ppermute | solution.py:569
  190.6 0.8 collective-permute-start.31
  191.4 1.1 collective-permute-start.32
  192.5 3.1 %collective-permute-done.31.refs_2_ = f32[32,512]{1,0:T(8,128)S(1)} collective-permute-done((f32[32,512]{1,0:T(8,128)S(1)}, f32[32,512]{1,0:T(8,128)S(1)}, u32[]{:S(2)}, u32[]{:S(2)}) %collective-permute-start.31) | collective-permute-done | bytes 65568 | tf_op jit(solution)/shard_map/ppermute | solution.py:569
  196.1 3.4 %left_factors.1 = (f32[128,512]{1,0:T(8,128)S(1)}, f32[40,512]{1,0:T(8,128)S(1)}, f32[8,120]{1,0:T(8,128)}, f32[8,480]{1,0:T(8,128)}, f32[8,1152]{1,0:T(8,128)S(...) custom-call(s32[1]{0:T(128)} %bitcast.group, f32[32,512]{1,0:T(8,128)S(1)} %add_add_fusion.refs_0_, ...), custom_call_target="tpu_custom_call" | custom-call | tf_op jit(solution)/shard_map/left_factors/pallas_call | solution.py:844
  199.8 0.8 collective-permute-start.34
  200.7 0.8 collective-permute-start.35
  201.7 2.0 collective-permute-done.34
  203.8 0.5 collective-permute-done.35
  204.3 0.6 collective-permute-start.36
  204.9 3.4 %collective-permute-done.36 = f32[8,1152]{1,0:T(8,128)S(1)} collective-permute-done((f32[8,1152]{1,0:T(8,128)S(1)}, f32[8,1152]{1,0:T(8,128)S(1)}, u32[]{:S(2)}, u32[]{:S(2)}) %collective-permute-start.36) | collective-permute-done | bytes 36896 | tf_op jit(solution)/shard_map/ppermute | solution.py:569
  208.3 1.2 collective-permute-start.37
  209.5 1.8 collective-permute-start.38
  211.3 1.4 collective-permute-start.39
  212.7 2.5 %collective-permute-done.38 = f32[8,1152]{1,0:T(8,128)S(1)} collective-permute-done((f32[8,1152]{1,0:T(8,128)S(1)}, f32[8,1152]{1,0:T(8,128)S(1)}, u32[]{:S(2)}, u32[]{:S(2)}) %collective-permute-start.38) | collective-permute-done | bytes 36896 | tf_op jit(solution)/shard_map/ppermute | solution.py:569
  215.2 1.9 collective-permute-done.39
  217.2 0.9 collective-permute-start.41
  218.1 1.0 collective-permute-start.42
  219.1 2.3 %collective-permute-done.41.refs_2_ = f32[8,1152]{1,0:T(8,128)S(1)} collective-permute-done((f32[8,1152]{1,0:T(8,128)S(1)}, f32[8,1152]{1,0:T(8,128)S(1)}, u32[]{:S(2)}, u32[]{:S(2)}) %collective-permute-start.41) | collective-permute-done | bytes 36896 | tf_op jit(solution)/shard_map/ppermute | solution.py:569
  221.9 5.5 %finish.1 = (f32[1,1]{1,0:T(1,128)}, f32[1,1]{1,0:T(1,128)}, f32[1,1]{1,0:T(1,128)}, f32[8,3840]{1,0:T(8,128)}, f32[8,480]{1,0:T(8,128)}, /*index=5*/f32[120,384...) custom-call(s32[1]{0:T(128)} %bitcast.group, ...), custom_call_target="tpu_custom_call" | custom-call | tf_op jit(solution)/shard_map/finish/pallas_call | solution.py:873
  (168 shorter events, 5.3 us)
Async XLA Ops:
  2.5 11.9 %collective-permute-start = (bf16[120,1440]{1,0:T(8,128)(2,1)S(1)}, bf16[120,1440]{1,0:T(8,128)(2,1)}, u32[]{:S(2)}, u32[]{:S(2)}) collective-permute-start(bf16[120,1440]{1,0:T(8,128)(2,1)S(1)} %slice.15.refs_0_), channel_id=1, source_target_pairs={{0,2},{1,3},{2,0},{3,1},{4,6},{5,7},{6,4},{7,5},{8,10},{9,11},{10,... | collective-permute-start | bytes 1036808 | tf_op jit(solution)/shard_map/ppermute | solution.py:569
  6.8 6.9 %collective-permute-start.1 = (f32[8,128]{1,0:T(8,128)S(1)}, f32[8,128]{1,0:T(8,128)S(1)}, u32[]{:S(2)}, u32[]{:S(2)}) collective-permute-start(f32[8,128]{1,0:T(8,128)S(1)} %broadcast_in_dim.33), channel_id=1, source_target_pairs={{0,1},{1,0},{2,3},{3,2},{4,5},{5,4},{6,7},{7,6},{8,9},{9,8},{10,11... | collective-permute-start | bytes 12296 | tf_op jit(solution)/shard_map/ppermute | solution.py:569
  14.4 4.4 %collective-permute-start.2 = (bf16[120,1440]{1,0:T(8,128)(2,1)S(1)}, bf16[120,1440]{1,0:T(8,128)(2,1)S(1)}, u32[]{:S(2)}, u32[]{:S(2)}) collective-permute-start(bf16[120,1440]{1,0:T(8,128)(2,1)S(1)} %slice.15.refs_0_), channel_id=1, source_target_pairs={{0,1},{1,0},{2,3},{3,2},{4,5},{5,4},{6,7},{7,6},{8,9},{9,8},{10,11... | collective-permute-start | bytes 1036808 | tf_op jit(solution)/shard_map/ppermute | solution.py:569
  15.0 3.8 %collective-permute-start.3 = (bf16[120,1440]{1,0:T(8,128)(2,1)}, bf16[120,1440]{1,0:T(8,128)(2,1)S(1)}, u32[]{:S(2)}, u32[]{:S(2)}) collective-permute-start(bf16[120,1440]{1,0:T(8,128)(2,1)} %collective-permute-done.refs_2_), channel_id=1, source_target_pairs={{0,1},{1,0},{2,3},{3,2},{4,5},{5,4},{6,7},{7,6},{8,9},{9,8},{10,11... | collective-permute-start | bytes 1036808 | tf_op jit(solution)/shard_map/ppermute | solution.py:569
  15.1 32.1 %copy-start.46 = (bf16[120,2400]{1,0:T(8,128)(2,1)}, bf16[120,2400]{1,0:T(8,128)(2,1)S(1)}, u32[]{:S(2)}) copy-start(bf16[120,2400]{1,0:T(8,128)(2,1)S(1)} %pad_maximum_fusion.refs_0_) | copy-start | bytes 1728004
  15.1 3.7 %collective-permute-start.4 = (f32[8,128]{1,0:T(8,128)S(1)}, f32[8,128]{1,0:T(8,128)S(1)}, u32[]{:S(2)}, u32[]{:S(2)}) collective-permute-start(f32[8,128]{1,0:T(8,128)S(1)} %broadcast_add_fusion), channel_id=1, source_target_pairs={{0,2},{1,3},{2,0},{3,1},{4,6},{5,7},{6,4},{7,5},{8,10},{9,11},{10,... | collective-permute-start | bytes 12296 | tf_op jit(solution)/shard_map/ppermute | solution.py:569
  16.7 31.1 %copy-start.47 = (bf16[480,480]{1,0:T(8,128)(2,1)}, bf16[480,480]{1,0:T(8,128)(2,1)S(1)}, u32[]{:S(2)}) copy-start(bf16[480,480]{1,0:T(8,128)(2,1)S(1)} %bitcast_convert_fusion.refs_4_) | copy-start | bytes 1382404
  18.8 28.4 %collective-permute-start.7 = (bf16[120,2400]{1,0:T(8,128)(2,1)S(1)}, bf16[120,2400]{1,0:T(8,128)(2,1)S(1)}, u32[]{:S(2)}, u32[]{:S(2)}) collective-permute-start(bf16[120,2400]{1,0:T(8,128)(2,1)S(1)} %pad_maximum_fusion.refs_0_), channel_id=1, source_target_pairs={{0,2},{1,3},{2,0},{3,1},{4,6},{5,7},{6,4},{7,5},{8,10},{9,11},{10,... | collective-permute-start | bytes 1728008 | tf_op jit(solution)/shard_map/ppermute | solution.py:569
  20.3 26.9 %collective-permute-start.8 = (bf16[480,480]{1,0:T(8,128)(2,1)S(1)}, bf16[480,480]{1,0:T(8,128)(2,1)S(1)}, u32[]{:S(2)}, u32[]{:S(2)}) collective-permute-start(bf16[480,480]{1,0:T(8,128)(2,1)S(1)} %bitcast_convert_fusion.refs_4_), channel_id=1, source_target_pairs={{0,2},{1,3},{2,0},{3,1},{4,6},{5,7},{6,4},{7,5},{8,10},{9,11},{10,... | collective-permute-start | bytes 1382408 | tf_op jit(solution)/shard_map/ppermute | solution.py:569
  20.9 6.3 %collective-permute-start.5 = (f32[8,128]{1,0:T(8,128)S(1)}, f32[8,128]{1,0:T(8,128)S(1)}, u32[]{:S(2)}, u32[]{:S(2)}) collective-permute-start(f32[8,128]{1,0:T(8,128)S(1)} %add.61), channel_id=1, source_target_pairs={{0,4},{4,0},{8,12},{12,8},{16,20},{20,16},{24,28},{28,24},{1,5},{5... | collective-permute-start | bytes 12296 | tf_op jit(solution)/shard_map/ppermute | solution.py:569
  27.2 19.9 %collective-permute-start.6 = (f32[8,128]{1,0:T(8,128)S(1)}, f32[8,128]{1,0:T(8,128)S(1)}, u32[]{:S(2)}, u32[]{:S(2)}) collective-permute-start(f32[8,128]{1,0:T(8,128)S(1)} %add.62), channel_id=1, source_target_pairs={{0,8},{4,12},{8,0},{12,4},{16,24},{20,28},{24,16},{28,20},{1,9},{5... | collective-permute-start | bytes 12296 | tf_op jit(solution)/shard_map/ppermute | solution.py:569
  47.2 21.4 %copy-start.17 = (f32[240,1024]{1,0:T(8,128)}, f32[240,1024]{1,0:T(8,128)S(1)}, u32[]{:S(2)}) copy-start(f32[240,1024]{1,0:T(8,128)S(1)} %get-tuple-element.157.mixa_ref) | copy-start | bytes 2949124
  47.2 21.3 %copy-start.52 = (bf16[480,480]{1,0:T(8,128)(2,1)}, bf16[480,480]{1,0:T(8,128)(2,1)S(1)}, u32[]{:S(2)}) copy-start(bf16[480,480]{1,0:T(8,128)(2,1)S(1)} %collective-permute-done.8.refs_6_) | copy-start | bytes 1382404
  47.2 21.3 %copy-start.48 = (bf16[120,2400]{1,0:T(8,128)(2,1)}, bf16[120,2400]{1,0:T(8,128)(2,1)S(1)}, u32[]{:S(2)}) copy-start(bf16[120,2400]{1,0:T(8,128)(2,1)S(1)} %collective-permute-done.7.refs_2_) | copy-start | bytes 1728004
  47.2 23.5 %collective-permute-start.10 = (bf16[120,2400]{1,0:T(8,128)(2,1)S(1)}, bf16[120,2400]{1,0:T(8,128)(2,1)S(1)}, u32[]{:S(2)}, u32[]{:S(2)}) collective-permute-start(bf16[120,2400]{1,0:T(8,128)(2,1)S(1)} %pad_maximum_fusion.refs_0_), channel_id=1, source_target_pairs={{0,1},{1,0},{2,3},{3,2},{4,5},{5,4},{6,7},{7,6},{8,9},{9,8},{10,11... | collective-permute-start | bytes 1728008 | tf_op jit(solution)/shard_map/ppermute | solution.py:569
  47.3 23.4 %collective-permute-start.11 = (bf16[120,2400]{1,0:T(8,128)(2,1)S(1)}, bf16[120,2400]{1,0:T(8,128)(2,1)S(1)}, u32[]{:S(2)}, u32[]{:S(2)}) collective-permute-start(bf16[120,2400]{1,0:T(8,128)(2,1)S(1)} %collective-permute-done.7.refs_2_), channel_id=1, source_target_pairs={{0,1},{1,0},{2,3},{3,2},{4,5},{5,4},{6,7},{7,6},{8,9},{9,8},{10,11... | collective-permute-start | bytes 1728008 | tf_op jit(solution)/shard_map/ppermute | solution.py:569
  47.8 22.9 %collective-permute-start.12 = (bf16[480,480]{1,0:T(8,128)(2,1)S(1)}, bf16[480,480]{1,0:T(8,128)(2,1)S(1)}, u32[]{:S(2)}, u32[]{:S(2)}) collective-permute-start(bf16[480,480]{1,0:T(8,128)(2,1)S(1)} %bitcast_convert_fusion.refs_4_), channel_id=1, source_target_pairs={{0,1},{1,0},{2,3},{3,2},{4,5},{5,4},{6,7},{7,6},{8,9},{9,8},{10,11... | collective-permute-start | bytes 1382408 | tf_op jit(solution)/shard_map/ppermute | solution.py:569
  47.9 22.8 %collective-permute-start.13 = (bf16[480,480]{1,0:T(8,128)(2,1)S(1)}, bf16[480,480]{1,0:T(8,128)(2,1)S(1)}, u32[]{:S(2)}, u32[]{:S(2)}) collective-permute-start(bf16[480,480]{1,0:T(8,128)(2,1)S(1)} %collective-permute-done.8.refs_6_), channel_id=1, source_target_pairs={{0,1},{1,0},{2,3},{3,2},{4,5},{5,4},{6,7},{7,6},{8,9},{9,8},{10,11... | collective-permute-start | bytes 1382408 | tf_op jit(solution)/shard_map/ppermute | solution.py:569
  48.3 21.8 %collective-permute-start.9 = (f32[8,128]{1,0:T(8,128)S(1)}, f32[8,128]{1,0:T(8,128)S(1)}, u32[]{:S(2)}, u32[]{:S(2)}) collective-permute-start(f32[8,128]{1,0:T(8,128)S(1)} %add.63), channel_id=1, source_target_pairs={{0,16},{4,20},{8,24},{12,28},{16,0},{20,4},{24,8},{28,12},{1,17},{... | collective-permute-start | bytes 12296 | tf_op jit(solution)/shard_map/ppermute | solution.py:569
  106.1 3.5 %collective-permute-start.14 = (bf16[480,480]{1,0:T(8,128)(2,1)}, bf16[480,480]{1,0:T(8,128)(2,1)S(1)}, u32[]{:S(2)}, u32[]{:S(2)}) collective-permute-start(bf16[480,480]{1,0:T(8,128)(2,1)} %get-tuple-element.180.refs_13_), channel_id=1, source_target_pairs={{0,1},{1,0},{2,3},{3,2},{4,5},{5,4},{6,7},{7,6},{8,9},{9,8},{10,11... | collective-permute-start | bytes 1382408 | tf_op jit(solution)/shard_map/ppermute | solution.py:569
  106.2 51.3 %collective-permute-start.17 = (bf16[120,2400]{1,0:T(8,128)(2,1)}, bf16[120,2400]{1,0:T(8,128)(2,1)S(1)}, u32[]{:S(2)}, u32[]{:S(2)}) collective-permute-start(bf16[120,2400]{1,0:T(8,128)(2,1)} %get-tuple-element.184.refs_9_), channel_id=1, source_target_pairs={{0,1},{1,0},{2,3},{3,2},{4,5},{5,4},{6,7},{7,6},{8,9},{9,8},{10,11... | collective-permute-start | bytes 1728008 | tf_op jit(solution)/shard_map/ppermute | solution.py:569
  106.7 50.8 %collective-permute-start.18 = (bf16[120,2400]{1,0:T(8,128)(2,1)}, bf16[120,2400]{1,0:T(8,128)(2,1)S(1)}, u32[]{:S(2)}, u32[]{:S(2)}) collective-permute-start(bf16[120,2400]{1,0:T(8,128)(2,1)} %get-tuple-element.185.refs_10_), channel_id=1, source_target_pairs={{0,2},{1,3},{2,0},{3,1},{4,6},{5,7},{6,4},{7,5},{8,10},{9,11},{10,... | collective-permute-start | bytes 1728008 | tf_op jit(solution)/shard_map/ppermute | solution.py:569
  108.1 49.4 %collective-permute-start.19 = (bf16[120,2400]{1,0:T(8,128)(2,1)}, bf16[120,2400]{1,0:T(8,128)(2,1)S(1)}, u32[]{:S(2)}, u32[]{:S(2)}) collective-permute-start(bf16[120,2400]{1,0:T(8,128)(2,1)} %get-tuple-element.186.refs_11_), channel_id=1, source_target_pairs={{0,3},{1,2},{2,1},{3,0},{4,7},{5,6},{6,5},{7,4},{8,11},{9,10},{10,... | collective-permute-start | bytes 1728008 | tf_op jit(solution)/shard_map/ppermute | solution.py:569
  108.1 49.3 %collective-permute-start.15 = (bf16[480,480]{1,0:T(8,128)(2,1)}, bf16[480,480]{1,0:T(8,128)(2,1)S(1)}, u32[]{:S(2)}, u32[]{:S(2)}) collective-permute-start(bf16[480,480]{1,0:T(8,128)(2,1)} %get-tuple-element.181.refs_14_), channel_id=1, source_target_pairs={{0,2},{1,3},{2,0},{3,1},{4,6},{5,7},{6,4},{7,5},{8,10},{9,11},{10,... | collective-permute-start | bytes 1382408 | tf_op jit(solution)/shard_map/ppermute | solution.py:569
  109.6 47.9 %collective-permute-start.16 = (bf16[480,480]{1,0:T(8,128)(2,1)}, bf16[480,480]{1,0:T(8,128)(2,1)S(1)}, u32[]{:S(2)}, u32[]{:S(2)}) collective-permute-start(bf16[480,480]{1,0:T(8,128)(2,1)} %get-tuple-element.182.refs_15_), channel_id=1, source_target_pairs={{0,3},{1,2},{2,1},{3,0},{4,7},{5,6},{6,5},{7,4},{8,11},{9,10},{10,... | collective-permute-start | bytes 1382408 | tf_op jit(solution)/shard_map/ppermute | solution.py:569
  111.5 46.0 %copy-start.3 = (f32[1024,480]{1,0:T(8,128)S(1)}, f32[1024,480]{1,0:T(8,128)}, u32[]{:S(2)}) copy-start(f32[1024,480]{1,0:T(8,128)} %copy-done.2) | copy-start | bytes 5898244
  111.5 46.0 %copy-start.8 = (f32[1024,480]{1,0:T(8,128)S(1)}, f32[1024,480]{1,0:T(8,128)}, u32[]{:S(2)}) copy-start(f32[1024,480]{1,0:T(8,128)} %get-tuple-element.192.dx_ref) | copy-start | bytes 5898244
  111.5 46.1 %copy-start.13 = (f32[1,3840,8]{1,2,0:T(8,128)S(1)}, f32[1,3840,8]{1,2,0:T(8,128)}, u32[]{:S(2)}) copy-start(f32[1,3840,8]{1,2,0:T(8,128)} %param.30) | copy-start | bytes 368644
  111.5 46.1 %copy-start.15 = (bf16[496,1024]{1,0:T(8,128)(2,1)S(1)}, bf16[496,1024]{1,0:T(8,128)(2,1)}, u32[]{:S(2)}) copy-start(bf16[496,1024]{1,0:T(8,128)(2,1)} %copy-done.14) | copy-start | bytes 3047428
  111.5 46.1 %copy-start.20 = (f32[1,6240]{1,0:T(1,128)S(1)}, f32[1,6240]{1,0:T(1,128)}, u32[]{:S(2)}) copy-start(f32[1,6240]{1,0:T(1,128)} %refs_16_.1) | copy-start | bytes 74884
  111.5 46.1 %copy-start.31 = (f32[56,512]{1,0:T(8,128)S(1)}, f32[56,512]{1,0:T(8,128)}, u32[]{:S(2)}) copy-start(f32[56,512]{1,0:T(8,128)} %get-tuple-element.195.e_ref) | copy-start | bytes 344068
  111.5 46.1 %copy-start.34 = (f32[40,512]{1,0:T(8,128)S(1)}, f32[40,512]{1,0:T(8,128)}, u32[]{:S(2)}) copy-start(f32[40,512]{1,0:T(8,128)} %get-tuple-element.193.s_ref) | copy-start | bytes 245764
  167.5 2.7 %collective-permute-start.25 = (bf16[120,1440]{1,0:T(8,128)(2,1)S(1)}, bf16[120,1440]{1,0:T(8,128)(2,1)S(1)}, u32[]{:S(2)}, u32[]{:S(2)}) collective-permute-start(bf16[120,1440]{1,0:T(8,128)(2,1)S(1)} %get-tuple-element.211.refs_7_), channel_id=1, source_target_pairs={{0,1},{1,0},{2,3},{3,2},{4,5},{5,4},{6,7},{7,6},{8,9},{9,8},{10,11... | collective-permute-start | bytes 1036808 | tf_op jit(solution)/shard_map/ppermute | solution.py:569
  167.7 4.5 %collective-permute-start.20 = (f32[32,512]{1,0:T(8,128)S(1)}, f32[32,512]{1,0:T(8,128)S(1)}, u32[]{:S(2)}, u32[]{:S(2)}) collective-permute-start(f32[32,512]{1,0:T(8,128)S(1)} %get-tuple-element.197), channel_id=1, source_target_pairs={{0,1},{1,0},{2,3},{3,2},{4,5},{5,4},{6,7},{7,6},{8,9},{9,8},{10,11... | collective-permute-start | bytes 196616 | tf_op jit(solution)/shard_map/ppermute | solution.py:569
  168.0 4.3 %collective-permute-start.21 = (f32[32,512]{1,0:T(8,128)S(1)}, f32[32,512]{1,0:T(8,128)S(1)}, u32[]{:S(2)}, u32[]{:S(2)}) collective-permute-start(f32[32,512]{1,0:T(8,128)S(1)} %get-tuple-element.198), channel_id=1, source_target_pairs={{0,2},{1,3},{2,0},{3,1},{4,6},{5,7},{6,4},{7,5},{8,10},{9,11},{10,... | collective-permute-start | bytes 196616 | tf_op jit(solution)/shard_map/ppermute | solution.py:569
  169.5 4.4 %collective-permute-start.22 = (f32[32,512]{1,0:T(8,128)S(1)}, f32[32,512]{1,0:T(8,128)S(1)}, u32[]{:S(2)}, u32[]{:S(2)}) collective-permute-start(f32[32,512]{1,0:T(8,128)S(1)} %get-tuple-element.199), channel_id=1, source_target_pairs={{0,3},{1,2},{2,1},{3,0},{4,7},{5,6},{6,5},{7,4},{8,11},{9,10},{10,... | collective-permute-start | bytes 196616 | tf_op jit(solution)/shard_map/ppermute | solution.py:569
  169.6 8.7 %collective-permute-start.24 = (bf16[120,1440]{1,0:T(8,128)(2,1)S(1)}, bf16[120,1440]{1,0:T(8,128)(2,1)S(1)}, u32[]{:S(2)}, u32[]{:S(2)}) collective-permute-start(bf16[120,1440]{1,0:T(8,128)(2,1)S(1)} %get-tuple-element.209.refs_5_), channel_id=1, source_target_pairs={{0,1},{1,0},{2,3},{3,2},{4,5},{5,4},{6,7},{7,6},{8,9},{9,8},{10,11... | collective-permute-start | bytes 1036808 | tf_op jit(solution)/shard_map/ppermute | solution.py:569
  170.3 11.5 %collective-permute-start.26 = (bf16[120,1440]{1,0:T(8,128)(2,1)S(1)}, bf16[120,1440]{1,0:T(8,128)(2,1)S(1)}, u32[]{:S(2)}, u32[]{:S(2)}) collective-permute-start(bf16[120,1440]{1,0:T(8,128)(2,1)S(1)} %add_convert_fusion), channel_id=1, source_target_pairs={{0,2},{1,3},{2,0},{3,1},{4,6},{5,7},{6,4},{7,5},{8,10},{9,11},{10,... | collective-permute-start | bytes 1036808 | tf_op jit(solution)/shard_map/ppermute | solution.py:569
  173.9 4.3 %collective-permute-start.23 = (f32[32,512]{1,0:T(8,128)S(1)}, f32[32,512]{1,0:T(8,128)S(1)}, u32[]{:S(2)}, u32[]{:S(2)}) collective-permute-start(f32[32,512]{1,0:T(8,128)S(1)} %add_add_fusion.1), channel_id=1, source_target_pairs={{0,4},{4,0},{8,12},{12,8},{16,20},{20,16},{24,28},{28,24},{1,5},{5... | collective-permute-start | bytes 196616 | tf_op jit(solution)/shard_map/ppermute | solution.py:569
  181.9 5.0 %collective-permute-start.27 = (f32[32,512]{1,0:T(8,128)S(1)}, f32[32,512]{1,0:T(8,128)S(1)}, u32[]{:S(2)}, u32[]{:S(2)}) collective-permute-start(f32[32,512]{1,0:T(8,128)S(1)} %add.69), channel_id=1, source_target_pairs={{0,8},{4,12},{8,0},{12,4},{16,24},{20,28},{24,16},{28,20},{1,9},{5... | collective-permute-start | bytes 196616 | tf_op jit(solution)/shard_map/ppermute | solution.py:569
  182.4 8.1 %collective-permute-start.28 = (f32[32,512]{1,0:T(8,128)S(1)}, f32[32,512]{1,0:T(8,128)S(1)}, u32[]{:S(2)}, u32[]{:S(2)}) collective-permute-start(f32[32,512]{1,0:T(8,128)S(1)} %add.69), channel_id=1, source_target_pairs={{0,16},{4,20},{8,24},{12,28},{16,0},{20,4},{24,8},{28,12},{1,17},{... | collective-permute-start | bytes 196616 | tf_op jit(solution)/shard_map/ppermute | solution.py:569
  182.7 7.9 %collective-permute-start.29 = (f32[32,512]{1,0:T(8,128)S(1)}, f32[32,512]{1,0:T(8,128)S(1)}, u32[]{:S(2)}, u32[]{:S(2)}) collective-permute-start(f32[32,512]{1,0:T(8,128)S(1)} %add.69), channel_id=1, source_target_pairs={{0,24},{4,28},{8,16},{12,20},{16,8},{20,12},{24,0},{28,4},{1,25},{... | collective-permute-start | bytes 196616 | tf_op jit(solution)/shard_map/ppermute | solution.py:569
  190.6 1.9 collective-permute-start.30
  190.6 5.0 %collective-permute-start.31 = (f32[32,512]{1,0:T(8,128)S(1)}, f32[32,512]{1,0:T(8,128)S(1)}, u32[]{:S(2)}, u32[]{:S(2)}) collective-permute-start(f32[32,512]{1,0:T(8,128)S(1)} %add_add_fusion.refs_0_), channel_id=1, source_target_pairs={{0,2},{1,3},{2,0},{3,1},{4,6},{5,7},{6,4},{7,5},{8,10},{9,11},{10,... | collective-permute-start | bytes 196616 | tf_op jit(solution)/shard_map/ppermute | solution.py:569
  191.4 4.7 %collective-permute-start.32 = (f32[32,512]{1,0:T(8,128)S(1)}, f32[32,512]{1,0:T(8,128)S(1)}, u32[]{:S(2)}, u32[]{:S(2)}) collective-permute-start(f32[32,512]{1,0:T(8,128)S(1)} %add_add_fusion.refs_0_), channel_id=1, source_target_pairs={{0,3},{1,2},{2,1},{3,0},{4,7},{5,6},{6,5},{7,4},{8,11},{9,10},{10,... | collective-permute-start | bytes 196616 | tf_op jit(solution)/shard_map/ppermute | solution.py:569
  196.1 25.7 %copy-start.10 = (f32[1,120,3840]{2,1,0:T(8,128)S(1)}, f32[1,120,3840]{2,1,0:T(8,128)}, u32[]{:S(2)}) copy-start(f32[1,120,3840]{2,1,0:T(8,128)} %param.26) | copy-start | bytes 5529604
  199.5 2.2 collective-permute-start.33
  199.8 4.0 %collective-permute-start.34 = (f32[8,1152]{1,0:T(8,128)S(1)}, f32[8,1152]{1,0:T(8,128)S(1)}, u32[]{:S(2)}, u32[]{:S(2)}) collective-permute-start(f32[8,1152]{1,0:T(8,128)S(1)} %get-tuple-element.222), channel_id=1, source_target_pairs={{0,2},{1,3},{2,0},{3,1},{4,6},{5,7},{6,4},{7,5},{8,10},{9,11},{10,... | collective-permute-start | bytes 110600 | tf_op jit(solution)/shard_map/ppermute | solution.py:569
  200.6 21.2 %copy-start.16 = (f32[1,480,480]{2,1,0:T(8,128)S(1)}, f32[1,480,480]{2,1,0:T(8,128)}, u32[]{:S(2)}) copy-start(f32[1,480,480]{2,1,0:T(8,128)} %param.27) | copy-start | bytes 2764804
  200.6 21.2 %copy-start.29 = (f32[481,33]{0,1:T(8,128)S(1)}, f32[481,33]{0,1:T(8,128)}, u32[]{:S(2)}) copy-start(f32[481,33]{0,1:T(8,128)} %param.38) | copy-start | bytes 190480
  200.6 21.2 %copy-start.32 = (f32[33,480]{1,0:T(8,128)S(1)}, f32[33,480]{1,0:T(8,128)}, u32[]{:S(2)}) copy-start(f32[33,480]{1,0:T(8,128)} %refs_21_.1) | copy-start | bytes 190084
  200.6 21.2 %copy-start.33 = (f32[481,33]{0,1:T(8,128)S(1)}, f32[481,33]{0,1:T(8,128)}, u32[]{:S(2)}) copy-start(f32[481,33]{0,1:T(8,128)} %param.39) | copy-start | bytes 190480
  200.6 21.2 %copy-start.38 = (f32[8,128]{1,0:T(8,128)S(1)}, f32[8,128]{1,0:T(8,128)}, u32[]{:S(2)}) copy-start(f32[8,128]{1,0:T(8,128)} %add.64.count_ref.refs_15_) | copy-start | bytes 12292
  200.6 21.2 %copy-start.39 = (f32[1,6240]{1,0:T(1,128)S(1)}, f32[1,6240]{1,0:T(1,128)}, u32[]{:S(2)}) copy-start(f32[1,6240]{1,0:T(1,128)} %refs_17_.1) | copy-start | bytes 74884
  200.7 21.2 %copy-start.41 = (f32[8,480]{1,0:T(8,128)S(1)}, f32[8,480]{1,0:T(8,128)}, u32[]{:S(2)}) copy-start(f32[8,480]{1,0:T(8,128)} %get-tuple-element.234.refs_7_) | copy-start | bytes 46084
  200.7 21.2 %copy-start.42 = (f32[2,480]{1,0:T(2,128)S(1)}, f32[2,480]{1,0:T(2,128)}, u32[]{:S(2)}) copy-start(f32[2,480]{1,0:T(2,128)} %refs_18_.1) | copy-start | bytes 11524
  200.7 3.6 %collective-permute-start.35 = (f32[8,1152]{1,0:T(8,128)S(1)}, f32[8,1152]{1,0:T(8,128)S(1)}, u32[]{:S(2)}, u32[]{:S(2)}) collective-permute-start(f32[8,1152]{1,0:T(8,128)S(1)} %get-tuple-element.223), channel_id=1, source_target_pairs={{0,3},{1,2},{2,1},{3,0},{4,7},{5,6},{6,5},{7,4},{8,11},{9,10},{10,... | collective-permute-start | bytes 110600 | tf_op jit(solution)/shard_map/ppermute | solution.py:569
  204.3 4.0 %collective-permute-start.36 = (f32[8,1152]{1,0:T(8,128)S(1)}, f32[8,1152]{1,0:T(8,128)S(1)}, u32[]{:S(2)}, u32[]{:S(2)}) collective-permute-start(f32[8,1152]{1,0:T(8,128)S(1)} %add_add_fusion.3), channel_id=1, source_target_pairs={{0,4},{4,0},{8,12},{12,8},{16,20},{20,16},{24,28},{28,24},{1,5},{5... | collective-permute-start | bytes 110600 | tf_op jit(solution)/shard_map/ppermute | solution.py:569
  208.3 4.4 %collective-permute-start.37 = (f32[8,1152]{1,0:T(8,128)S(1)}, f32[8,1152]{1,0:T(8,128)S(1)}, u32[]{:S(2)}, u32[]{:S(2)}) collective-permute-start(f32[8,1152]{1,0:T(8,128)S(1)} %add.76), channel_id=1, source_target_pairs={{0,8},{4,12},{8,0},{12,4},{16,24},{20,28},{24,16},{28,20},{1,9},{5... | collective-permute-start | bytes 110600 | tf_op jit(solution)/shard_map/ppermute | solution.py:569
  209.5 5.6 %collective-permute-start.38 = (f32[8,1152]{1,0:T(8,128)S(1)}, f32[8,1152]{1,0:T(8,128)S(1)}, u32[]{:S(2)}, u32[]{:S(2)}) collective-permute-start(f32[8,1152]{1,0:T(8,128)S(1)} %add.76), channel_id=1, source_target_pairs={{0,16},{4,20},{8,24},{12,28},{16,0},{20,4},{24,8},{28,12},{1,17},{... | collective-permute-start | bytes 110600 | tf_op jit(solution)/shard_map/ppermute | solution.py:569
  211.3 5.8 %collective-permute-start.39 = (f32[8,1152]{1,0:T(8,128)S(1)}, f32[8,1152]{1,0:T(8,128)S(1)}, u32[]{:S(2)}, u32[]{:S(2)}) collective-permute-start(f32[8,1152]{1,0:T(8,128)S(1)} %add.76), channel_id=1, source_target_pairs={{0,24},{4,28},{8,16},{12,20},{16,8},{20,12},{24,0},{28,4},{1,25},{... | collective-permute-start | bytes 110600 | tf_op jit(solution)/shard_map/ppermute | solution.py:569
  217.1 1.9 collective-permute-start.40
  217.2 4.2 %collective-permute-start.41 = (f32[8,1152]{1,0:T(8,128)S(1)}, f32[8,1152]{1,0:T(8,128)S(1)}, u32[]{:S(2)}, u32[]{:S(2)}) collective-permute-start(f32[8,1152]{1,0:T(8,128)S(1)} %add_add_fusion.2.refs_0_), channel_id=1, source_target_pairs={{0,2},{1,3},{2,0},{3,1},{4,6},{5,7},{6,4},{7,5},{8,10},{9,11},{10,... | collective-permute-start | bytes 110600 | tf_op jit(solution)/shard_map/ppermute | solution.py:569
  218.1 3.7 %collective-permute-start.42 = (f32[8,1152]{1,0:T(8,128)S(1)}, f32[8,1152]{1,0:T(8,128)S(1)}, u32[]{:S(2)}, u32[]{:S(2)}) collective-permute-start(f32[8,1152]{1,0:T(8,128)S(1)} %add_add_fusion.2.refs_0_), channel_id=1, source_target_pairs={{0,3},{1,2},{2,1},{3,0},{4,7},{5,6},{6,5},{7,4},{8,11},{9,10},{10,... | collective-permute-start | bytes 110600 | tf_op jit(solution)/shard_map/ppermute | solution.py:569
  (36 other events, 324.4 us)

commit v2 on v1

--- a/solution.py
+++ b/solution.py
@@ -585,6 +585,12 @@
     return [pieces[0]] + [swap(piece, "grp", place) for place, piece in enumerate(pieces) if place]
 
 
+def moves_of(axis):
+    first, *bits = bits_of(axis)
+    pairs = [[first]] + [bits[at : at + 2] for at in range(0, len(bits), 2)]
+    return [pair + [sum(pair)] * (len(pair) - 1) for pair in pairs]
+
+
 def add_chunks(pieces, work=()):
     work, results = dict(work), {}
 
@@ -597,9 +603,7 @@
     total = got[0]
     for piece in got[1:]:
         total = total + piece
-    first, *bits = bits_of("rep")
-    for turn, pair in enumerate([[first]] + [bits[at : at + 2] for at in range(0, len(bits), 2)]):
-        moves = pair + [sum(pair)] * (len(pair) - 1)
+    for turn, moves in enumerate(moves_of("rep")):
         for piece in beside(turn + 1, [swap(total, "rep", move) for move in moves]):
             total = total + piece
     got = [total] + [swap(total, "grp", place) for place in range(1, len(pieces))]
@@ -675,11 +679,13 @@
         )
 
     shape = jax.ShapeDtypeStruct
-    rounds = [("grp", bit) for bit in bits_of("grp")] + [("rep", bit) for bit in bits_of("rep")]
+    rounds = [("grp", [bit]) for bit in bits_of("grp")] + [("rep", moves) for moves in moves_of("rep")]
 
     def advance(value, times=1):
         for _ in range(min(times, len(rounds))):
-            value = value + swap(value, *rounds.pop(0))
+            axis, moves = rounds.pop(0)
+            for piece in [swap(value, axis, move) for move in moves]:
+                value = value + piece
         return value
 
     cols = pl.BlockSpec((1, step), lambda i, *_: (0, i))
@@ -710,8 +716,7 @@
     w_in = gather_end(w_in)
     rest = jnp.concatenate([mats_d[0][:, 4 * D :], mats_d[0][:, 3 * D : 4 * D]], 1).astype(B16)
     down = mats_down[0].astype(B16)
-    more = advance(counted)
-    w_in, counted, rest, down = tie(w_in, more, rest, down)
+    w_in, counted, rest, down = tie(w_in, counted, rest, down)
     w_rest, w_down = gather_start(rest), gather_start(down)
     more = advance(counted)
     query, keys, value = call(

time: 228 us -> 254 us (1.11)
  waiting for transfers between devices: 31.5 us -> 56.1 us
    ppermute x43 -> x44, waiting for transfers between devices: 31.5 us -> 56.1 us  [swap(): return lax.ppermute(value, axis, [(i, i ^ bit) for i in range(size)])]
    unnamed x112 -> x118, local copies, waits for them, and re-layouts: 7.66 us -> 9.06 us
    ppermute x43 -> x44, starting transfers between devices: 38.2 us -> 37.9 us  [swap(): return lax.ppermute(value, axis, [(i, i ^ bit) for i in range(size)])]
  transfers between devices with their start and end apart: 43 -> 44, of which waited for: 15 -> 18; matrix products, arithmetic and copies ran while one was open for 2% -> 2% of each run, Pallas kernels for 40% -> 36%
where the time goes in v2:
time: 254 us
  Pallas kernels  143 us (56%)
  waiting for transfers between devices  56.1 us (22%)
  starting transfers between devices  37.9 us (15%)
  local copies, waits for them, and re-layouts  10.5 us (4%)
  other arithmetic  4.65 us (2%)
    ppermute x44, waiting for transfers between devices, swap(): return lax.ppermute(value, axis, [(i, i ^ bit) for i in range(size)])  56.1 us
    pallas_call x1, Pallas kernels, shards(): pl.pallas_call(attend_back_kernel, grid=(HEADS // pair,), in_specs=[pl.Bl...  46 us
    ppermute x44, starting transfers between devices, swap(): return lax.ppermute(value, axis, [(i, i ^ bit) for i in range(size)])  37.9 us
    pallas_call x2, Pallas kernels, shards(): pl.pallas_call(attend_kernel, grid=(half,), in_specs=[one, one, one] + [p...  35.3 us
    pallas_call x1, Pallas kernels, shards(): call(partial(middle_kernel, members), 'feed_and_loss', (length // step_mi...  33.6 us
    pallas_call x1, Pallas kernels, shards(): call(partial(input_kernel, members), 'input_grads', (steps,), [cols, act,...  9.85 us
    unnamed x118, local copies, waits for them, and re-layouts  9.06 us
    pallas_call x1, Pallas kernels, shards(): call(partial(finish_kernel, members, replicas), 'finish', (1,), [whole(it...  5.46 us
  transfers between devices with their start and end apart: 44, of which 18 were waited for; matrix products, arithmetic and copies ran while one was open for 2% of the time, Pallas kernels for 36%

profile of v2, /device:TPU:0, one launch (start us, length us, event | category | flops | bytes accessed | tf_op | source)
XLA Modules:
  0.0 253.8 jit_solution(7575276955810021940)
XLA Ops:
  0.7 1.7 bitcast_convert_fusion.1
  2.5 3.0 %collective-permute-start = (bf16[120,1440]{1,0:T(8,128)(2,1)S(1)}, bf16[120,1440]{1,0:T(8,128)(2,1)}, u32[]{:S(2)}, u32[]{:S(2)}) collective-permute-start(bf16[120,1440]{1,0:T(8,128)(2,1)S(1)} %slice.15.refs_0_), channel_id=1, source_target_pairs={{0,2},{1,3},{2,0},{3,1},{4,6},{5,7},{6,4},{7,5},{8,10},{9,11},{10,... | collective-permute-start | bytes 1036808 | tf_op jit(solution)/shard_map/ppermute | solution.py:569
  5.5 0.6 convert_reduce_fusion
  6.1 0.6 broadcast_in_dim.33
  6.8 0.8 bitcast_convert_fusion.refs_4_
  7.7 0.8 slice.17
  8.4 2.2 embed.1
  10.7 1.3 copy-done.2
  12.0 1.0 copy-done.14
  12.9 0.7 copy-done.38
  13.7 1.5 error_sketch.1.serr_ref
  15.2 0.7 broadcast_add_fusion
  16.6 1.2 collective-permute-done.2.refs_1_
  17.8 0.7 collective-permute-done.3.refs_3_
  19.0 1.5 collective-permute-start.7
  21.0 4.7 %project.1 = (bf16[20,32,1024]{2,1,0:T(8,128)(2,1)S(1)}, bf16[20,32,1024]{2,1,0:T(8,128)(2,1)S(1)}, bf16[20,32,1024]{2,1,0:T(8,128)(2,1)S(1)}) custom-call(s32[1]{0:T(128)} %bitcast.group, bf16[1024,480]{1,0:T(8,128)(2,1)S(1)} %get-tuple-element.140.h_ref, bf16[120,1440]{1,0:T(8,128)(2,1)S(1)} %slice.15.refs_0_, ...), custom_call_target="tpu_custom_call" | custom-call | tf_op jit(solution)/shard_map/project/pallas_call | solution.py:722
  25.8 18.8 %collective-permute-done.4 = f32[8,128]{1,0:T(8,128)S(1)} collective-permute-done((f32[8,128]{1,0:T(8,128)S(1)}, f32[8,128]{1,0:T(8,128)S(1)}, u32[]{:S(2)}, u32[]{:S(2)}) %collective-permute-start.4) | collective-permute-done | bytes 4128 | tf_op jit(solution)/shard_map/ppermute | solution.py:569
  44.6 1.5 collective-permute-start.5
  46.1 17.7 %attend.2 = (f32[240,1024]{1,0:T(8,128)S(1)}, f32[10,1,1024]{2,1,0:T(1,128)S(1)}, bf16[20,1024,1024]{2,1,0:T(8,128)(2,1)}) custom-call(bf16[20,32,1024]{2,1,0:T(8,128)(2,1)S(1)} %get-tuple-element.188.q_ref, bf16[20,32,1024]{2,1,0:T(8,128)(2,1)S(1)} %get-tuple-element.151.k_ref, bf16[20,32,1024]{2,1,0:T(8,128)(2,1)S(1)} %get-tuple-element.152.v_ref), custom_call_target="tpu_custom_call" | custom-call | tf_op jit(solution)/shard_map/attend/pallas_call | solution.py:737
  63.8 0.6 copy-done.39
  65.5 3.6 %collective-permute-start.10 = (f32[8,128]{1,0:T(8,128)S(1)}, f32[8,128]{1,0:T(8,128)S(1)}, u32[]{:S(2)}, u32[]{:S(2)}) collective-permute-start(f32[8,128]{1,0:T(8,128)S(1)} %add.65), channel_id=1, source_target_pairs={{0,24},{4,28},{8,16},{12,20},{16,8},{20,12},{24,0},{28,4},{1,25},{... | collective-permute-start | bytes 12296 | tf_op jit(solution)/shard_map/ppermute | solution.py:569
  69.1 1.8 collective-permute-done.10
  70.9 3.6 %collective-permute-done.8 = f32[8,128]{1,0:T(8,128)S(1)} collective-permute-done((f32[8,128]{1,0:T(8,128)S(1)}, f32[8,128]{1,0:T(8,128)S(1)}, u32[]{:S(2)}, u32[]{:S(2)}) %collective-permute-start.8) | collective-permute-done | bytes 4128 | tf_op jit(solution)/shard_map/ppermute | solution.py:569
  74.5 2.1 collective-permute-start.9
  76.7 17.6 %attend.3 = (f32[240,1024]{1,0:T(8,128)S(1)}, f32[10,1,1024]{2,1,0:T(1,128)S(1)}, bf16[20,1024,1024]{2,1,0:T(8,128)(2,1)}) custom-call(bf16[20,32,1024]{2,1,0:T(8,128)(2,1)S(1)} %get-tuple-element.188.q_ref, bf16[20,32,1024]{2,1,0:T(8,128)(2,1)S(1)} %get-tuple-element.151.k_ref, ...), custom_call_target="tpu_custom_call", output_to_operand_aliasing={{2}: (3, {})} | custom-call | tf_op jit(solution)/shard_map/attend/pallas_call | solution.py:737
  94.3 0.9 copy-done.18
  95.3 0.6 copy-done.40
  95.9 0.6 add_add_fusion.4.count_ref.refs_15_
  96.5 0.8 copy-done.52
  97.4 0.8 copy-done.53
  98.2 33.6 %feed_and_loss.1 = (bf16[20,32,1024]{2,1,0:T(8,128)(2,1)}, f32[1024,480]{1,0:T(8,128)}, f32[40,512]{1,0:T(8,128)}, f32[56,512]{1,0:T(8,128)}, bf16[120,2400]{1,0...) custom-call(s32[1]{0:T(128)} %bitcast.group, ...), custom_call_target="tpu_custom_call" | custom-call | tf_op jit(solution)/shard_map/feed_and_loss/pallas_call | solution.py:765
  133.0 0.9 collective-permute-start.20
  133.9 0.6 collective-permute-start.16
  134.5 1.4 collective-permute-start.17
  136.0 1.3 copy-done.11
  137.4 46.0 %attend_back.1.da_ref = bf16[3,480,1024]{2,1,0:T(8,128)(2,1)S(1)} custom-call(bf16[20,1024,1024]{2,1,0:T(8,128)(2,1)} %get-tuple-element.187.p_ref, bf16[20,32,1024]{2,1,0:T(8,128)(2,1)S(1)} %get-tuple-element.188.q_ref, bf16[20,32,1024]{2,1,0:T(8,128)(2,1)S(1)} %get-tuple-element.151.k_ref, bf16[20,32,1024]{2,1,0:T(8,128)(2,1)S(1)} %get-tuple-element.152.v_ref, ...), custom_call_target="tpu_custom_call" | custom-call | tf_op jit(solution)/shard_map/attend_back/pallas_call | solution.py:800
  183.5 9.9 %input_grads.1 = (bf16[120,1440]{1,0:T(8,128)(2,1)S(1)}, bf16[120,1440]{1,0:T(8,128)(2,1)S(1)}, bf16[120,1440]{1,0:T(8,128)(2,1)S(1)}, bf16[120,1440]{1,0:T(8,12...) custom-call(s32[1]{0:T(128)} %bitcast.group, ...), custom_call_target="tpu_custom_call" | custom-call | tf_op jit(solution)/shard_map/input_grads/pallas_call | solution.py:817
  194.4 0.9 collective-permute-start.23
  195.3 0.7 collective-permute-start.25
  197.0 1.8 collective-permute-done.22
  198.8 0.6 collective-permute-start.24
  199.4 4.3 %collective-permute-done.24 = f32[32,512]{1,0:T(8,128)S(1)} collective-permute-done((f32[32,512]{1,0:T(8,128)S(1)}, f32[32,512]{1,0:T(8,128)S(1)}, u32[]{:S(2)}, u32[]{:S(2)}) %collective-permute-start.24) | collective-permute-done | bytes 65568 | tf_op jit(solution)/shard_map/ppermute | solution.py:569
  203.7 3.7 %collective-permute-done.27.refs_2_ = bf16[120,1440]{1,0:T(8,128)(2,1)S(1)} collective-permute-done((bf16[120,1440]{1,0:T(8,128)(2,1)S(1)}, bf16[120,1440]{1,0:T(8,128)(2,1)S(1)}, u32[]{:S(2)}, u32[]{:S(2)}) %collective-permute-start.27) | collective-permute-done | bytes 345632 | tf_op jit(solution)/shard_map/ppermute | solution.py:569
  207.5 2.1 collective-permute-start.28
  209.6 2.4 collective-permute-start.30
  212.6 4.1 %collective-permute-done.29 = f32[32,512]{1,0:T(8,128)S(1)} collective-permute-done((f32[32,512]{1,0:T(8,128)S(1)}, f32[32,512]{1,0:T(8,128)S(1)}, u32[]{:S(2)}, u32[]{:S(2)}) %collective-permute-start.29) | collective-permute-done | bytes 65568 | tf_op jit(solution)/shard_map/ppermute | solution.py:569
  216.9 1.2 collective-permute-start.32
  218.0 0.7 collective-permute-start.33
  218.7 3.1 %collective-permute-done.32.refs_2_ = f32[32,512]{1,0:T(8,128)S(1)} collective-permute-done((f32[32,512]{1,0:T(8,128)S(1)}, f32[32,512]{1,0:T(8,128)S(1)}, u32[]{:S(2)}, u32[]{:S(2)}) %collective-permute-start.32) | collective-permute-done | bytes 65568 | tf_op jit(solution)/shard_map/ppermute | solution.py:569
  222.4 3.4 %left_factors.1 = (f32[128,512]{1,0:T(8,128)S(1)}, f32[40,512]{1,0:T(8,128)S(1)}, f32[8,120]{1,0:T(8,128)}, f32[8,480]{1,0:T(8,128)}, f32[8,1152]{1,0:T(8,128)S(...) custom-call(s32[1]{0:T(128)} %bitcast.group, f32[32,512]{1,0:T(8,128)S(1)} %add_add_fusion.refs_0_, ...), custom_call_target="tpu_custom_call" | custom-call | tf_op jit(solution)/shard_map/left_factors/pallas_call | solution.py:849
  226.0 1.1 collective-permute-start.35
  228.0 2.0 collective-permute-done.35
  230.0 1.0 collective-permute-done.36
  230.9 0.6 collective-permute-start.37
  231.6 3.4 %collective-permute-done.37 = f32[8,1152]{1,0:T(8,128)S(1)} collective-permute-done((f32[8,1152]{1,0:T(8,128)S(1)}, f32[8,1152]{1,0:T(8,128)S(1)}, u32[]{:S(2)}, u32[]{:S(2)}) %collective-permute-start.37) | collective-permute-done | bytes 36896 | tf_op jit(solution)/shard_map/ppermute | solution.py:569
  235.0 1.7 collective-permute-start.38
  236.7 2.6 %collective-permute-start.40 = (f32[8,1152]{1,0:T(8,128)S(1)}, f32[8,1152]{1,0:T(8,128)S(1)}, u32[]{:S(2)}, u32[]{:S(2)}) collective-permute-start(f32[8,1152]{1,0:T(8,128)S(1)} %add.80), channel_id=1, source_target_pairs={{0,24},{4,28},{8,16},{12,20},{16,8},{20,12},{24,0},{28,4},{1,25},{... | collective-permute-start | bytes 110600 | tf_op jit(solution)/shard_map/ppermute | solution.py:569
  239.4 2.3 collective-permute-done.39
  241.7 0.8 collective-permute-done.40
  242.6 1.4 collective-permute-start.42
  244.4 2.2 collective-permute-done.42.refs_2_
  246.6 0.8 collective-permute-done.43.refs_3_
  247.5 0.7 copy-done.47
  248.2 5.5 %finish.1 = (f32[1,1]{1,0:T(1,128)}, f32[1,1]{1,0:T(1,128)}, f32[1,1]{1,0:T(1,128)}, f32[8,3840]{1,0:T(8,128)}, f32[8,480]{1,0:T(8,128)}, /*index=5*/f32[120,384...) custom-call(s32[1]{0:T(128)} %bitcast.group, ...), custom_call_target="tpu_custom_call" | custom-call | tf_op jit(solution)/shard_map/finish/pallas_call | solution.py:878
  (175 shorter events, 9.3 us)
Async XLA Ops:
  2.5 13.4 %collective-permute-start = (bf16[120,1440]{1,0:T(8,128)(2,1)S(1)}, bf16[120,1440]{1,0:T(8,128)(2,1)}, u32[]{:S(2)}, u32[]{:S(2)}) collective-permute-start(bf16[120,1440]{1,0:T(8,128)(2,1)S(1)} %slice.15.refs_0_), channel_id=1, source_target_pairs={{0,2},{1,3},{2,0},{3,1},{4,6},{5,7},{6,4},{7,5},{8,10},{9,11},{10,... | collective-permute-start | bytes 1036808 | tf_op jit(solution)/shard_map/ppermute | solution.py:569
  6.8 8.4 %collective-permute-start.1 = (f32[8,128]{1,0:T(8,128)S(1)}, f32[8,128]{1,0:T(8,128)S(1)}, u32[]{:S(2)}, u32[]{:S(2)}) collective-permute-start(f32[8,128]{1,0:T(8,128)S(1)} %broadcast_in_dim.33), channel_id=1, source_target_pairs={{0,1},{1,0},{2,3},{3,2},{4,5},{5,4},{6,7},{7,6},{8,9},{9,8},{10,11... | collective-permute-start | bytes 12296 | tf_op jit(solution)/shard_map/ppermute | solution.py:569
  15.9 1.9 collective-permute-start.2
  16.4 2.1 collective-permute-start.3
  16.6 47.9 %copy-start.49 = (bf16[120,2400]{1,0:T(8,128)(2,1)}, bf16[120,2400]{1,0:T(8,128)(2,1)S(1)}, u32[]{:S(2)}) copy-start(bf16[120,2400]{1,0:T(8,128)(2,1)S(1)} %pad_maximum_fusion.refs_0_) | copy-start | bytes 1728004
  18.5 45.9 %collective-permute-start.6 = (bf16[120,2400]{1,0:T(8,128)(2,1)S(1)}, bf16[120,2400]{1,0:T(8,128)(2,1)S(1)}, u32[]{:S(2)}, u32[]{:S(2)}) collective-permute-start(bf16[120,2400]{1,0:T(8,128)(2,1)S(1)} %pad_maximum_fusion.refs_0_), channel_id=1, source_target_pairs={{0,2},{1,3},{2,0},{3,1},{4,6},{5,7},{6,4},{7,5},{8,10},{9,11},{10,... | collective-permute-start | bytes 1728008 | tf_op jit(solution)/shard_map/ppermute | solution.py:569
  19.0 45.4 %collective-permute-start.7 = (bf16[480,480]{1,0:T(8,128)(2,1)S(1)}, bf16[480,480]{1,0:T(8,128)(2,1)S(1)}, u32[]{:S(2)}, u32[]{:S(2)}) collective-permute-start(bf16[480,480]{1,0:T(8,128)(2,1)S(1)} %copy-done.50), channel_id=1, source_target_pairs={{0,2},{1,3},{2,0},{3,1},{4,6},{5,7},{6,4},{7,5},{8,10},{9,11},{10,... | collective-permute-start | bytes 1382408 | tf_op jit(solution)/shard_map/ppermute | solution.py:569
  20.5 24.0 %collective-permute-start.4 = (f32[8,128]{1,0:T(8,128)S(1)}, f32[8,128]{1,0:T(8,128)S(1)}, u32[]{:S(2)}, u32[]{:S(2)}) collective-permute-start(f32[8,128]{1,0:T(8,128)S(1)} %broadcast_add_fusion), channel_id=1, source_target_pairs={{0,2},{1,3},{2,0},{3,1},{4,6},{5,7},{6,4},{7,5},{8,10},{9,11},{10,... | collective-permute-start | bytes 12296 | tf_op jit(solution)/shard_map/ppermute | solution.py:569
  44.6 19.8 %collective-permute-start.5 = (f32[8,128]{1,0:T(8,128)S(1)}, f32[8,128]{1,0:T(8,128)S(1)}, u32[]{:S(2)}, u32[]{:S(2)}) collective-permute-start(f32[8,128]{1,0:T(8,128)S(1)} %add.64), channel_id=1, source_target_pairs={{0,4},{4,0},{8,12},{12,8},{16,20},{20,16},{24,28},{28,24},{1,5},{5... | collective-permute-start | bytes 12296 | tf_op jit(solution)/shard_map/ppermute | solution.py:569
  64.4 29.9 %copy-start.17 = (f32[240,1024]{1,0:T(8,128)}, f32[240,1024]{1,0:T(8,128)S(1)}, u32[]{:S(2)}) copy-start(f32[240,1024]{1,0:T(8,128)S(1)} %get-tuple-element.157.mixa_ref) | copy-start | bytes 2949124
  64.4 29.9 %copy-start.55 = (bf16[480,480]{1,0:T(8,128)(2,1)}, bf16[480,480]{1,0:T(8,128)(2,1)S(1)}, u32[]{:S(2)}) copy-start(bf16[480,480]{1,0:T(8,128)(2,1)S(1)} %collective-permute-done.7.refs_6_) | copy-start | bytes 1382404
  64.4 29.9 %copy-start.51 = (bf16[120,2400]{1,0:T(8,128)(2,1)}, bf16[120,2400]{1,0:T(8,128)(2,1)S(1)}, u32[]{:S(2)}) copy-start(bf16[120,2400]{1,0:T(8,128)(2,1)S(1)} %collective-permute-done.6.refs_2_) | copy-start | bytes 1728004
  64.4 32.1 %collective-permute-start.11 = (bf16[120,2400]{1,0:T(8,128)(2,1)S(1)}, bf16[120,2400]{1,0:T(8,128)(2,1)S(1)}, u32[]{:S(2)}, u32[]{:S(2)}) collective-permute-start(bf16[120,2400]{1,0:T(8,128)(2,1)S(1)} %pad_maximum_fusion.refs_0_), channel_id=1, source_target_pairs={{0,1},{1,0},{2,3},{3,2},{4,5},{5,4},{6,7},{7,6},{8,9},{9,8},{10,11... | collective-permute-start | bytes 1728008 | tf_op jit(solution)/shard_map/ppermute | solution.py:569
  64.5 32.0 %collective-permute-start.12 = (bf16[120,2400]{1,0:T(8,128)(2,1)S(1)}, bf16[120,2400]{1,0:T(8,128)(2,1)S(1)}, u32[]{:S(2)}, u32[]{:S(2)}) collective-permute-start(bf16[120,2400]{1,0:T(8,128)(2,1)S(1)} %collective-permute-done.6.refs_2_), channel_id=1, source_target_pairs={{0,1},{1,0},{2,3},{3,2},{4,5},{5,4},{6,7},{7,6},{8,9},{9,8},{10,11... | collective-permute-start | bytes 1728008 | tf_op jit(solution)/shard_map/ppermute | solution.py:569
  65.0 31.5 %collective-permute-start.13 = (bf16[480,480]{1,0:T(8,128)(2,1)S(1)}, bf16[480,480]{1,0:T(8,128)(2,1)S(1)}, u32[]{:S(2)}, u32[]{:S(2)}) collective-permute-start(bf16[480,480]{1,0:T(8,128)(2,1)S(1)} %copy-done.50), channel_id=1, source_target_pairs={{0,1},{1,0},{2,3},{3,2},{4,5},{5,4},{6,7},{7,6},{8,9},{9,8},{10,11... | collective-permute-start | bytes 1382408 | tf_op jit(solution)/shard_map/ppermute | solution.py:569
  65.1 31.4 %collective-permute-start.14 = (bf16[480,480]{1,0:T(8,128)(2,1)S(1)}, bf16[480,480]{1,0:T(8,128)(2,1)S(1)}, u32[]{:S(2)}, u32[]{:S(2)}) collective-permute-start(bf16[480,480]{1,0:T(8,128)(2,1)S(1)} %collective-permute-done.7.refs_6_), channel_id=1, source_target_pairs={{0,1},{1,0},{2,3},{3,2},{4,5},{5,4},{6,7},{7,6},{8,9},{9,8},{10,11... | collective-permute-start | bytes 1382408 | tf_op jit(solution)/shard_map/ppermute | solution.py:569
  65.5 5.4 %collective-permute-start.10 = (f32[8,128]{1,0:T(8,128)S(1)}, f32[8,128]{1,0:T(8,128)S(1)}, u32[]{:S(2)}, u32[]{:S(2)}) collective-permute-start(f32[8,128]{1,0:T(8,128)S(1)} %add.65), channel_id=1, source_target_pairs={{0,24},{4,28},{8,16},{12,20},{16,8},{20,12},{24,0},{28,4},{1,25},{... | collective-permute-start | bytes 12296 | tf_op jit(solution)/shard_map/ppermute | solution.py:569
  70.9 3.6 %collective-permute-start.8 = (f32[8,128]{1,0:T(8,128)S(1)}, f32[8,128]{1,0:T(8,128)S(1)}, u32[]{:S(2)}, u32[]{:S(2)}) collective-permute-start(f32[8,128]{1,0:T(8,128)S(1)} %add.65), channel_id=1, source_target_pairs={{0,8},{4,12},{8,0},{12,4},{16,24},{20,28},{24,16},{28,20},{1,9},{5... | collective-permute-start | bytes 12296 | tf_op jit(solution)/shard_map/ppermute | solution.py:569
  74.5 21.3 %collective-permute-start.9 = (f32[8,128]{1,0:T(8,128)S(1)}, f32[8,128]{1,0:T(8,128)S(1)}, u32[]{:S(2)}, u32[]{:S(2)}) collective-permute-start(f32[8,128]{1,0:T(8,128)S(1)} %add.65), channel_id=1, source_target_pairs={{0,16},{4,20},{8,24},{12,28},{16,0},{20,4},{24,8},{28,12},{1,17},{... | collective-permute-start | bytes 12296 | tf_op jit(solution)/shard_map/ppermute | solution.py:569
  131.9 2.6 %collective-permute-start.15 = (bf16[480,480]{1,0:T(8,128)(2,1)}, bf16[480,480]{1,0:T(8,128)(2,1)S(1)}, u32[]{:S(2)}, u32[]{:S(2)}) collective-permute-start(bf16[480,480]{1,0:T(8,128)(2,1)} %get-tuple-element.180.refs_13_), channel_id=1, source_target_pairs={{0,1},{1,0},{2,3},{3,2},{4,5},{5,4},{6,7},{7,6},{8,9},{9,8},{10,11... | collective-permute-start | bytes 1382408 | tf_op jit(solution)/shard_map/ppermute | solution.py:569
  132.0 51.4 %collective-permute-start.18 = (bf16[120,2400]{1,0:T(8,128)(2,1)}, bf16[120,2400]{1,0:T(8,128)(2,1)S(1)}, u32[]{:S(2)}, u32[]{:S(2)}) collective-permute-start(bf16[120,2400]{1,0:T(8,128)(2,1)} %get-tuple-element.184.refs_9_), channel_id=1, source_target_pairs={{0,1},{1,0},{2,3},{3,2},{4,5},{5,4},{6,7},{7,6},{8,9},{9,8},{10,11... | collective-permute-start | bytes 1728008 | tf_op jit(solution)/shard_map/ppermute | solution.py:569
  132.5 50.9 %collective-permute-start.19 = (bf16[120,2400]{1,0:T(8,128)(2,1)}, bf16[120,2400]{1,0:T(8,128)(2,1)S(1)}, u32[]{:S(2)}, u32[]{:S(2)}) collective-permute-start(bf16[120,2400]{1,0:T(8,128)(2,1)} %get-tuple-element.185.refs_10_), channel_id=1, source_target_pairs={{0,2},{1,3},{2,0},{3,1},{4,6},{5,7},{6,4},{7,5},{8,10},{9,11},{10,... | collective-permute-start | bytes 1728008 | tf_op jit(solution)/shard_map/ppermute | solution.py:569
  133.0 50.4 %collective-permute-start.20 = (bf16[120,2400]{1,0:T(8,128)(2,1)}, bf16[120,2400]{1,0:T(8,128)(2,1)S(1)}, u32[]{:S(2)}, u32[]{:S(2)}) collective-permute-start(bf16[120,2400]{1,0:T(8,128)(2,1)} %get-tuple-element.186.refs_11_), channel_id=1, source_target_pairs={{0,3},{1,2},{2,1},{3,0},{4,7},{5,6},{6,5},{7,4},{8,11},{9,10},{10,... | collective-permute-start | bytes 1728008 | tf_op jit(solution)/shard_map/ppermute | solution.py:569
  133.9 49.4 %collective-permute-start.16 = (bf16[480,480]{1,0:T(8,128)(2,1)}, bf16[480,480]{1,0:T(8,128)(2,1)S(1)}, u32[]{:S(2)}, u32[]{:S(2)}) collective-permute-start(bf16[480,480]{1,0:T(8,128)(2,1)} %get-tuple-element.181.refs_14_), channel_id=1, source_target_pairs={{0,2},{1,3},{2,0},{3,1},{4,6},{5,7},{6,4},{7,5},{8,10},{9,11},{10,... | collective-permute-start | bytes 1382408 | tf_op jit(solution)/shard_map/ppermute | solution.py:569
  134.5 48.8 %collective-permute-start.17 = (bf16[480,480]{1,0:T(8,128)(2,1)}, bf16[480,480]{1,0:T(8,128)(2,1)S(1)}, u32[]{:S(2)}, u32[]{:S(2)}) collective-permute-start(bf16[480,480]{1,0:T(8,128)(2,1)} %get-tuple-element.182.refs_15_), channel_id=1, source_target_pairs={{0,3},{1,2},{2,1},{3,0},{4,7},{5,6},{6,5},{7,4},{8,11},{9,10},{10,... | collective-permute-start | bytes 1382408 | tf_op jit(solution)/shard_map/ppermute | solution.py:569
  137.3 46.1 %copy-start.3 = (f32[1024,480]{1,0:T(8,128)S(1)}, f32[1024,480]{1,0:T(8,128)}, u32[]{:S(2)}) copy-start(f32[1024,480]{1,0:T(8,128)} %copy-done.2) | copy-start | bytes 5898244
  137.3 46.1 %copy-start.8 = (f32[1024,480]{1,0:T(8,128)S(1)}, f32[1024,480]{1,0:T(8,128)}, u32[]{:S(2)}) copy-start(f32[1024,480]{1,0:T(8,128)} %get-tuple-element.192.dx_ref) | copy-start | bytes 5898244
  137.3 46.1 %copy-start.13 = (f32[1,3840,8]{1,2,0:T(8,128)S(1)}, f32[1,3840,8]{1,2,0:T(8,128)}, u32[]{:S(2)}) copy-start(f32[1,3840,8]{1,2,0:T(8,128)} %param.30) | copy-start | bytes 368644
  137.3 46.1 %copy-start.15 = (bf16[496,1024]{1,0:T(8,128)(2,1)S(1)}, bf16[496,1024]{1,0:T(8,128)(2,1)}, u32[]{:S(2)}) copy-start(bf16[496,1024]{1,0:T(8,128)(2,1)} %copy-done.14) | copy-start | bytes 3047428
  137.3 46.1 %copy-start.20 = (f32[1,6240]{1,0:T(1,128)S(1)}, f32[1,6240]{1,0:T(1,128)}, u32[]{:S(2)}) copy-start(f32[1,6240]{1,0:T(1,128)} %refs_16_.1) | copy-start | bytes 74884
  137.3 46.1 %copy-start.31 = (f32[40,512]{1,0:T(8,128)S(1)}, f32[40,512]{1,0:T(8,128)}, u32[]{:S(2)}) copy-start(f32[40,512]{1,0:T(8,128)} %copy-done.30) | copy-start | bytes 245764
  137.3 46.1 %copy-start.34 = (f32[56,512]{1,0:T(8,128)S(1)}, f32[56,512]{1,0:T(8,128)}, u32[]{:S(2)}) copy-start(f32[56,512]{1,0:T(8,128)} %get-tuple-element.195.e_ref) | copy-start | bytes 344068
  137.3 46.1 %copy-start.37 = (f32[40,512]{1,0:T(8,128)S(1)}, f32[40,512]{1,0:T(8,128)}, u32[]{:S(2)}) copy-start(f32[40,512]{1,0:T(8,128)} %get-tuple-element.193.s_ref) | copy-start | bytes 245764
  193.3 2.7 %collective-permute-start.26 = (bf16[120,1440]{1,0:T(8,128)(2,1)S(1)}, bf16[120,1440]{1,0:T(8,128)(2,1)S(1)}, u32[]{:S(2)}, u32[]{:S(2)}) collective-permute-start(bf16[120,1440]{1,0:T(8,128)(2,1)S(1)} %get-tuple-element.211.refs_7_), channel_id=1, source_target_pairs={{0,1},{1,0},{2,3},{3,2},{4,5},{5,4},{6,7},{7,6},{8,9},{9,8},{10,11... | collective-permute-start | bytes 1036808 | tf_op jit(solution)/shard_map/ppermute | solution.py:569
  193.5 3.6 %collective-permute-start.21 = (f32[32,512]{1,0:T(8,128)S(1)}, f32[32,512]{1,0:T(8,128)S(1)}, u32[]{:S(2)}, u32[]{:S(2)}) collective-permute-start(f32[32,512]{1,0:T(8,128)S(1)} %get-tuple-element.197), channel_id=1, source_target_pairs={{0,1},{1,0},{2,3},{3,2},{4,5},{5,4},{6,7},{7,6},{8,9},{9,8},{10,11... | collective-permute-start | bytes 196616 | tf_op jit(solution)/shard_map/ppermute | solution.py:569
  193.9 4.9 %collective-permute-start.22 = (f32[32,512]{1,0:T(8,128)S(1)}, f32[32,512]{1,0:T(8,128)S(1)}, u32[]{:S(2)}, u32[]{:S(2)}) collective-permute-start(f32[32,512]{1,0:T(8,128)S(1)} %get-tuple-element.198), channel_id=1, source_target_pairs={{0,2},{1,3},{2,0},{3,1},{4,6},{5,7},{6,4},{7,5},{8,10},{9,11},{10,... | collective-permute-start | bytes 196616 | tf_op jit(solution)/shard_map/ppermute | solution.py:569
  194.4 4.4 %collective-permute-start.23 = (f32[32,512]{1,0:T(8,128)S(1)}, f32[32,512]{1,0:T(8,128)S(1)}, u32[]{:S(2)}, u32[]{:S(2)}) collective-permute-start(f32[32,512]{1,0:T(8,128)S(1)} %get-tuple-element.199), channel_id=1, source_target_pairs={{0,3},{1,2},{2,1},{3,0},{4,7},{5,6},{6,5},{7,4},{8,11},{9,10},{10,... | collective-permute-start | bytes 196616 | tf_op jit(solution)/shard_map/ppermute | solution.py:569
  195.3 8.4 %collective-permute-start.25 = (bf16[120,1440]{1,0:T(8,128)(2,1)S(1)}, bf16[120,1440]{1,0:T(8,128)(2,1)S(1)}, u32[]{:S(2)}, u32[]{:S(2)}) collective-permute-start(bf16[120,1440]{1,0:T(8,128)(2,1)S(1)} %get-tuple-element.209.refs_5_), channel_id=1, source_target_pairs={{0,1},{1,0},{2,3},{3,2},{4,5},{5,4},{6,7},{7,6},{8,9},{9,8},{10,11... | collective-permute-start | bytes 1036808 | tf_op jit(solution)/shard_map/ppermute | solution.py:569
  196.2 11.2 %collective-permute-start.27 = (bf16[120,1440]{1,0:T(8,128)(2,1)S(1)}, bf16[120,1440]{1,0:T(8,128)(2,1)S(1)}, u32[]{:S(2)}, u32[]{:S(2)}) collective-permute-start(bf16[120,1440]{1,0:T(8,128)(2,1)S(1)} %add_convert_fusion), channel_id=1, source_target_pairs={{0,2},{1,3},{2,0},{3,1},{4,6},{5,7},{6,4},{7,5},{8,10},{9,11},{10,... | collective-permute-start | bytes 1036808 | tf_op jit(solution)/shard_map/ppermute | solution.py:569
  198.8 4.9 %collective-permute-start.24 = (f32[32,512]{1,0:T(8,128)S(1)}, f32[32,512]{1,0:T(8,128)S(1)}, u32[]{:S(2)}, u32[]{:S(2)}) collective-permute-start(f32[32,512]{1,0:T(8,128)S(1)} %add_add_fusion.1), channel_id=1, source_target_pairs={{0,4},{4,0},{8,12},{12,8},{16,20},{20,16},{24,28},{28,24},{1,5},{5... | collective-permute-start | bytes 196616 | tf_op jit(solution)/shard_map/ppermute | solution.py:569
  207.5 5.1 %collective-permute-start.28 = (f32[32,512]{1,0:T(8,128)S(1)}, f32[32,512]{1,0:T(8,128)S(1)}, u32[]{:S(2)}, u32[]{:S(2)}) collective-permute-start(f32[32,512]{1,0:T(8,128)S(1)} %add.73), channel_id=1, source_target_pairs={{0,8},{4,12},{8,0},{12,4},{16,24},{20,28},{24,16},{28,20},{1,9},{5... | collective-permute-start | bytes 196616 | tf_op jit(solution)/shard_map/ppermute | solution.py:569
  209.6 7.2 %collective-permute-start.29 = (f32[32,512]{1,0:T(8,128)S(1)}, f32[32,512]{1,0:T(8,128)S(1)}, u32[]{:S(2)}, u32[]{:S(2)}) collective-permute-start(f32[32,512]{1,0:T(8,128)S(1)} %add.73), channel_id=1, source_target_pairs={{0,16},{4,20},{8,24},{12,28},{16,0},{20,4},{24,8},{28,12},{1,17},{... | collective-permute-start | bytes 196616 | tf_op jit(solution)/shard_map/ppermute | solution.py:569
  209.6 7.1 %collective-permute-start.30 = (f32[32,512]{1,0:T(8,128)S(1)}, f32[32,512]{1,0:T(8,128)S(1)}, u32[]{:S(2)}, u32[]{:S(2)}) collective-permute-start(f32[32,512]{1,0:T(8,128)S(1)} %add.73), channel_id=1, source_target_pairs={{0,24},{4,28},{8,16},{12,20},{16,8},{20,12},{24,0},{28,4},{1,25},{... | collective-permute-start | bytes 196616 | tf_op jit(solution)/shard_map/ppermute | solution.py:569
  216.8 1.9 collective-permute-start.31
  216.9 4.9 %collective-permute-start.32 = (f32[32,512]{1,0:T(8,128)S(1)}, f32[32,512]{1,0:T(8,128)S(1)}, u32[]{:S(2)}, u32[]{:S(2)}) collective-permute-start(f32[32,512]{1,0:T(8,128)S(1)} %add_add_fusion.refs_0_), channel_id=1, source_target_pairs={{0,2},{1,3},{2,0},{3,1},{4,6},{5,7},{6,4},{7,5},{8,10},{9,11},{10,... | collective-permute-start | bytes 196616 | tf_op jit(solution)/shard_map/ppermute | solution.py:569
  218.0 4.3 %collective-permute-start.33 = (f32[32,512]{1,0:T(8,128)S(1)}, f32[32,512]{1,0:T(8,128)S(1)}, u32[]{:S(2)}, u32[]{:S(2)}) collective-permute-start(f32[32,512]{1,0:T(8,128)S(1)} %add_add_fusion.refs_0_), channel_id=1, source_target_pairs={{0,3},{1,2},{2,1},{3,0},{4,7},{5,6},{6,5},{7,4},{8,11},{9,10},{10,... | collective-permute-start | bytes 196616 | tf_op jit(solution)/shard_map/ppermute | solution.py:569
  222.4 25.0 %copy-start.10 = (f32[1,120,3840]{2,1,0:T(8,128)S(1)}, f32[1,120,3840]{2,1,0:T(8,128)}, u32[]{:S(2)}) copy-start(f32[1,120,3840]{2,1,0:T(8,128)} %param.26) | copy-start | bytes 5529604
  222.4 25.0 %copy-start.46 = (f32[2,480]{1,0:T(2,128)S(1)}, f32[2,480]{1,0:T(2,128)}, u32[]{:S(2)}) copy-start(f32[2,480]{1,0:T(2,128)} %refs_19_.1) | copy-start | bytes 11524
  225.8 2.2 collective-permute-start.34
  226.0 4.0 %collective-permute-start.35 = (f32[8,1152]{1,0:T(8,128)S(1)}, f32[8,1152]{1,0:T(8,128)S(1)}, u32[]{:S(2)}, u32[]{:S(2)}) collective-permute-start(f32[8,1152]{1,0:T(8,128)S(1)} %get-tuple-element.222), channel_id=1, source_target_pairs={{0,2},{1,3},{2,0},{3,1},{4,6},{5,7},{6,4},{7,5},{8,10},{9,11},{10,... | collective-permute-start | bytes 110600 | tf_op jit(solution)/shard_map/ppermute | solution.py:569
  227.1 20.3 %copy-start.16 = (f32[1,480,480]{2,1,0:T(8,128)S(1)}, f32[1,480,480]{2,1,0:T(8,128)}, u32[]{:S(2)}) copy-start(f32[1,480,480]{2,1,0:T(8,128)} %param.27) | copy-start | bytes 2764804
  227.1 20.3 %copy-start.29 = (f32[481,33]{0,1:T(8,128)S(1)}, f32[481,33]{0,1:T(8,128)}, u32[]{:S(2)}) copy-start(f32[481,33]{0,1:T(8,128)} %param.38) | copy-start | bytes 190480
  227.1 20.3 %copy-start.33 = (f32[33,480]{1,0:T(8,128)S(1)}, f32[33,480]{1,0:T(8,128)}, u32[]{:S(2)}) copy-start(f32[33,480]{1,0:T(8,128)} %refs_20_.1) | copy-start | bytes 190084
  227.2 20.3 %copy-start.35 = (f32[33,480]{1,0:T(8,128)S(1)}, f32[33,480]{1,0:T(8,128)}, u32[]{:S(2)}) copy-start(f32[33,480]{1,0:T(8,128)} %refs_21_.1) | copy-start | bytes 190084
  227.2 20.3 %copy-start.36 = (f32[481,33]{0,1:T(8,128)S(1)}, f32[481,33]{0,1:T(8,128)}, u32[]{:S(2)}) copy-start(f32[481,33]{0,1:T(8,128)} %param.39) | copy-start | bytes 190480
  227.2 20.3 %copy-start.41 = (f32[8,128]{1,0:T(8,128)S(1)}, f32[8,128]{1,0:T(8,128)}, u32[]{:S(2)}) copy-start(f32[8,128]{1,0:T(8,128)} %add_add_fusion.4.count_ref.refs_15_) | copy-start | bytes 12292
  227.2 3.7 %collective-permute-start.36 = (f32[8,1152]{1,0:T(8,128)S(1)}, f32[8,1152]{1,0:T(8,128)S(1)}, u32[]{:S(2)}, u32[]{:S(2)}) collective-permute-start(f32[8,1152]{1,0:T(8,128)S(1)} %get-tuple-element.223), channel_id=1, source_target_pairs={{0,3},{1,2},{2,1},{3,0},{4,7},{5,6},{6,5},{7,4},{8,11},{9,10},{10,... | collective-permute-start | bytes 110600 | tf_op jit(solution)/shard_map/ppermute | solution.py:569
  230.9 4.0 %collective-permute-start.37 = (f32[8,1152]{1,0:T(8,128)S(1)}, f32[8,1152]{1,0:T(8,128)S(1)}, u32[]{:S(2)}, u32[]{:S(2)}) collective-permute-start(f32[8,1152]{1,0:T(8,128)S(1)} %add_add_fusion.3), channel_id=1, source_target_pairs={{0,4},{4,0},{8,12},{12,8},{16,20},{20,16},{24,28},{28,24},{1,5},{5... | collective-permute-start | bytes 110600 | tf_op jit(solution)/shard_map/ppermute | solution.py:569
  235.0 4.4 %collective-permute-start.38 = (f32[8,1152]{1,0:T(8,128)S(1)}, f32[8,1152]{1,0:T(8,128)S(1)}, u32[]{:S(2)}, u32[]{:S(2)}) collective-permute-start(f32[8,1152]{1,0:T(8,128)S(1)} %add.80), channel_id=1, source_target_pairs={{0,8},{4,12},{8,0},{12,4},{16,24},{20,28},{24,16},{28,20},{1,9},{5... | collective-permute-start | bytes 110600 | tf_op jit(solution)/shard_map/ppermute | solution.py:569
  236.7 5.0 %collective-permute-start.39 = (f32[8,1152]{1,0:T(8,128)S(1)}, f32[8,1152]{1,0:T(8,128)S(1)}, u32[]{:S(2)}, u32[]{:S(2)}) collective-permute-start(f32[8,1152]{1,0:T(8,128)S(1)} %add.80), channel_id=1, source_target_pairs={{0,16},{4,20},{8,24},{12,28},{16,0},{20,4},{24,8},{28,12},{1,17},{... | collective-permute-start | bytes 110600 | tf_op jit(solution)/shard_map/ppermute | solution.py:569
  236.7 5.8 %collective-permute-start.40 = (f32[8,1152]{1,0:T(8,128)S(1)}, f32[8,1152]{1,0:T(8,128)S(1)}, u32[]{:S(2)}, u32[]{:S(2)}) collective-permute-start(f32[8,1152]{1,0:T(8,128)S(1)} %add.80), channel_id=1, source_target_pairs={{0,24},{4,28},{8,16},{12,20},{16,8},{20,12},{24,0},{28,4},{1,25},{... | collective-permute-start | bytes 110600 | tf_op jit(solution)/shard_map/ppermute | solution.py:569
  242.5 1.9 collective-permute-start.41
  242.6 4.0 %collective-permute-start.42 = (f32[8,1152]{1,0:T(8,128)S(1)}, f32[8,1152]{1,0:T(8,128)S(1)}, u32[]{:S(2)}, u32[]{:S(2)}) collective-permute-start(f32[8,1152]{1,0:T(8,128)S(1)} %add_add_fusion.2.refs_0_), channel_id=1, source_target_pairs={{0,2},{1,3},{2,0},{3,1},{4,6},{5,7},{6,4},{7,5},{8,10},{9,11},{10,... | collective-permute-start | bytes 110600 | tf_op jit(solution)/shard_map/ppermute | solution.py:569
  243.9 3.4 %collective-permute-start.43 = (f32[8,1152]{1,0:T(8,128)S(1)}, f32[8,1152]{1,0:T(8,128)S(1)}, u32[]{:S(2)}, u32[]{:S(2)}) collective-permute-start(f32[8,1152]{1,0:T(8,128)S(1)} %add_add_fusion.2.refs_0_), channel_id=1, source_target_pairs={{0,3},{1,2},{2,1},{3,0},{4,7},{5,6},{6,5},{7,4},{8,11},{9,10},{10,... | collective-permute-start | bytes 110600 | tf_op jit(solution)/shard_map/ppermute | solution.py:569
  (40 other events, 329.4 us)
